TPU v7x, 32 devices: a whole 2x2x4 slice. The times are simulated.
32 devices in a mesh: lon: 8 (over z, y), lat: 4 (over x, core).
Axes of the slice: x: 2, y: 2, z: 4, core: 2. Of those that a mesh axis runs over, the one named last changes fastest.
Arguments:
- heat_content: float32 [1024, 2048], P('lat', 'lon'), may hold values from -6 to 6
- saltiness_anomaly: float32 [1024, 2048], P('lat', 'lon'), may hold values from -6 to 6
- water_indicator: int32 [1024, 2048], P('lat', 'lon'), may hold values 0 or 1
- gradient_kind_index: int32 [1024, 2048], P('lat', 'lon'), may hold values from 0 to 15
- gradient_kind_table: float32 [16, 2], replicated, may hold values from -1 to 1
- easterly_transit_number: float32 [1024, 2048], P('lat', 'lon'), may hold values from -0.5 to 0.5
- poleward_transit_number: float32 [1024, 2048], P('lat', 'lon'), may hold values from -0.5 to 0.5
Outputs:
- new_temperature: float32 [1024, 2048], P('lat', 'lon')
- new_salinity: float32 [1024, 2048], P('lat', 'lon')
All inputs are finite; a program needn't handle non-finite values. No bound on the sum of `water_indicator` on one device may be relied on, other than what follows from the above.
Results may differ from a plain program's by a relative error of at most 0.0003.
Values sent between devices are 32-bit elements; how exact they have to be, the bound alone decides.
A program may use at most 64 MiB of HBM per device.

v0:
```python
import jax
import jax.numpy as jnp
from jax import lax
from jax.sharding import PartitionSpec as P

STEPS = 4


def padded(block, sides, width, periodic):
    for axis, dim in sides:
        count = lax.axis_size(axis)
        forward = [(i, i + 1) for i in range(count - 1)]
        if periodic:
            forward.append((count - 1, 0))
        backward = [(target, source) for source, target in forward]
        low = lax.ppermute(
            lax.slice_in_dim(block, block.shape[dim] - width, None, axis=dim), axis, forward
        )
        high = lax.ppermute(lax.slice_in_dim(block, 0, width, axis=dim), axis, backward)
        block = jnp.concatenate([low, block, high], axis=dim)
    return block


def face_flux_terms(
    far_left_tracer,
    lower_tracer,
    upper_tracer,
    far_right_tracer,
    lower_tracer_northern,
    upper_tracer_northern,
    lower_tracer_southern,
    upper_tracer_southern,
    lower_mask,
    upper_mask,
    lower_velocity,
    upper_velocity,
    lower_slope_first,
    upper_slope_first,
    lower_slope_second,
    upper_slope_second,
):
    face_velocity = 0.5 * (lower_velocity + upper_velocity)
    downwind_value = upper_tracer - lower_tracer
    forward = face_velocity > 0
    du = jnp.where(forward, lower_tracer - far_left_tracer, far_right_tracer - upper_tracer)
    lim = jnp.where(
        downwind_value * du > 0,
        jnp.where(jnp.abs(downwind_value) < jnp.abs(du), downwind_value, du),
        0.0,
    )
    face_value = (
        jnp.where(forward, lower_tracer, upper_tracer)
        + jnp.where(forward, 0.5, -0.5) * (1.0 - jnp.abs(face_velocity)) * lim
    )
    first_slope = 0.5 * (lower_slope_first + upper_slope_first)
    second_slope = 0.5 * (lower_slope_second + upper_slope_second)
    cross_terms = 0.25 * (
        lower_tracer_northern
        + upper_tracer_northern
        - lower_tracer_southern
        - upper_tracer_southern
    )
    return (
        lower_mask
        * upper_mask
        * (
            0.1
            * (
                (1.0 + first_slope * first_slope) * downwind_value
                + first_slope * second_slope * cross_terms
            )
            - face_velocity * face_value
        )
    )


def advance(ext, stat):
    rows = ext.shape[1] - 4
    cols = ext.shape[2] - 4

    def win(a, r0, c0, nr, nc):
        return a[..., r0 : r0 + nr, c0 : c0 + nc]

    def xs(a, r0, c0):
        return win(a, r0, c0, rows, cols + 1)

    def ys(a, r0, c0):
        return win(a, r0, c0, rows + 1, cols)

    sea_mask, easterly_isoneutral_gradient, poleward_isoneutral_gradient, u_vel, v_vel = (
        stat[0],
        stat[1],
        stat[2],
        stat[3],
        stat[4],
    )
    east = face_flux_terms(
        xs(ext, 2, 0),
        xs(ext, 2, 1),
        xs(ext, 2, 2),
        xs(ext, 2, 3),
        xs(ext, 3, 1),
        xs(ext, 3, 2),
        xs(ext, 1, 1),
        xs(ext, 1, 2),
        xs(sea_mask, 2, 1),
        xs(sea_mask, 2, 2),
        xs(u_vel, 2, 1),
        xs(u_vel, 2, 2),
        xs(easterly_isoneutral_gradient, 2, 1),
        xs(easterly_isoneutral_gradient, 2, 2),
        xs(poleward_isoneutral_gradient, 2, 1),
        xs(poleward_isoneutral_gradient, 2, 2),
    )
    north = face_flux_terms(
        ys(ext, 0, 2),
        ys(ext, 1, 2),
        ys(ext, 2, 2),
        ys(ext, 3, 2),
        ys(ext, 1, 3),
        ys(ext, 2, 3),
        ys(ext, 1, 1),
        ys(ext, 2, 1),
        ys(sea_mask, 1, 2),
        ys(sea_mask, 2, 2),
        ys(v_vel, 1, 2),
        ys(v_vel, 2, 2),
        ys(poleward_isoneutral_gradient, 1, 2),
        ys(poleward_isoneutral_gradient, 2, 2),
        ys(easterly_isoneutral_gradient, 1, 2),
        ys(easterly_isoneutral_gradient, 2, 2),
    )
    centre = win(ext, 2, 2, rows, cols)
    sea = win(sea_mask, 2, 2, rows, cols)
    return sea * (centre + east[..., 1:] - east[..., :-1] + north[..., 1:, :] - north[..., :-1, :])


def mirror_rows(top_rows):
    every = lax.all_gather(top_rows[None], "lon", axis=0, tiled=True)
    partner = lax.axis_size("lon") - 1 - lax.axis_index("lon")
    mate = lax.dynamic_index_in_dim(every, partner, 0, keepdims=False)
    return mate[:, ::-1, ::-1]


def extend(stacked_fields, signs):
    nrows = stacked_fields.shape[1]
    sign_arr = jnp.array(signs, jnp.float32)[:, None, None]
    top_band = lax.axis_index("lat") == lax.axis_size("lat") - 1
    tall = padded(stacked_fields, (("lat", 1),), 2, False)
    ghost = mirror_rows(stacked_fields[:, nrows - 2 :, :]) * sign_arr
    upper = jnp.where(top_band, ghost, tall[:, nrows + 2 :, :])
    tall = jnp.concatenate([tall[:, : nrows + 2, :], upper], 1)
    return padded(tall, (("lon", 2),), 2, True)


def local(
    heat_content,
    saltiness_anomaly,
    water_indicator,
    gradient_kind_index,
    gradient_kind_table,
    easterly_transit_number,
    poleward_transit_number,
):
    sea_mask = water_indicator.astype(jnp.float32)
    easterly_isoneutral_gradient = jnp.zeros_like(heat_content)
    poleward_isoneutral_gradient = jnp.zeros_like(heat_content)
    for klass in range(gradient_kind_table.shape[0]):
        hit = gradient_kind_index == klass
        easterly_isoneutral_gradient = easterly_isoneutral_gradient + jnp.where(
            hit, gradient_kind_table[klass, 0], 0.0
        )
        poleward_isoneutral_gradient = poleward_isoneutral_gradient + jnp.where(
            hit, gradient_kind_table[klass, 1], 0.0
        )
    joined_rows = jnp.stack(
        [
            sea_mask,
            easterly_isoneutral_gradient,
            poleward_isoneutral_gradient,
            easterly_transit_number,
            poleward_transit_number,
            heat_content,
            saltiness_anomaly,
        ]
    )
    first = extend(joined_rows, (1.0, 1.0, 1.0, -1.0, -1.0, 1.0, 1.0))
    stat = first[:5]
    current = first[5:]
    transported_quantities = jnp.stack([heat_content, saltiness_anomaly])
    for step in range(STEPS):
        transported_quantities = advance(current, stat)
        if step + 1 < STEPS:
            current = extend(transported_quantities, (1.0, 1.0))
    return (transported_quantities[0], transported_quantities[1])


def solution(mesh):
    placed = (
        P("lat", "lon"),
        P("lat", "lon"),
        P("lat", "lon"),
        P("lat", "lon"),
        P(),
        P("lat", "lon"),
        P("lat", "lon"),
    )
    return jax.shard_map(
        local,
        mesh=mesh,
        in_specs=placed,
        out_specs=(P("lat", "lon"), P("lat", "lon")),
        check_vma=False,
    )
```

profile of v0, /device:TPU:1, one launch (start us, length us, event | category | flops | bytes accessed | tf_op | source)
XLA Modules:
  0.0 250.4 jit_solution(12331991262169018663)
XLA Ops:
  0.6 2.1 fusion.83
  2.7 1.8 fusion.84
  4.6 1.0 bitcast_dynamic-update-slice_fusion.4
  5.6 12.1 %bitcast_dynamic-update-slice_fusion.3 = (f32[7,256,256]{2,1,0:T(8,128)S(1)}, pred[256,256]{1,0:T(8,128)(4,1)S(1)}, pred[256,256]{1,0:T(8,128)(4,1)S(1)}, pred[2...) fusion(f32[7,256,256]{2,1,0:T(8,128)S(1)} %bitcast_dynamic-upda, ...), kind=kLoop, calls=%fused_computation.190 | loop fusion | flops 3080192 | bytes 1572928
  17.7 10.4 %bitcast_dynamic-update-slice_fusion.2 = f32[7,256,256]{2,1,0:T(8,128)S(1)} fusion(f32[7,256,256]{2,1,0:T(8,128)S(1)} %get-tuple-element.6, pred[256,256]{1,0:T(8,128)(4,1)S(1)} %get-tuple-element.22, pred[256,256]{1,0:T(8,128)(4,1)S(1)} %get-tuple-element.21, pred[256,256]{1,0:T(8,128)(4,1)S(1)} %get-tuple-element.20, ...), kind=kLoop, calls=%fused_computation.189 | loop fusion | flops 2031616 | bytes 1310784
  28.3 2.0 collective-permute-start.1
  30.3 4.5 %collective-permute-start = (f32[7,2,256]{2,1,0:T(2,128)S(1)}, f32[7,2,256]{2,1,0:T(2,128)S(1)}, u32[]{:S(2)}, u32[]{:S(2)}) collective-permute-start(f32[7,2,256]{2,1,0:T(2,128)S(1)} %get-tuple-element.32), channel_id=1, source_target_pairs={{0,1},{1,2},{2,3},{4,5},{5,6},{6,7},{8,9},{9,10},{10,11},{12,13},{... | collective-permute-start | bytes 43016 | tf_op jit(solution)/shard_map/ppermute | solution.py:16
  34.8 24.8 %all-gather = f32[56,2,256]{2,1,0:T(2,128)S(1)} all-gather(f32[7,2,256]{2,1,0:T(2,128)S(1)} %get-tuple-element.32), channel_id=2, replica_groups=mesh['lon'=8,'lat'=4] {'lon'}, dimensions={0}, use_global_device_ids=true | all-gather | bytes 129024 | tf_op jit(solution)/shard_map/all_gather | solution.py:139
  59.5 0.3 rev.12
  60.1 1.2 fusion.75
  61.3 1.6 copy.14
  62.9 3.9 %collective-permute-start.3 = (f32[7,260,2]{1,2,0:T(2,128)S(1)}, f32[7,260,2]{1,2,0:T(2,128)S(1)}, u32[]{:S(2)}, u32[]{:S(2)}) collective-permute-start(f32[7,260,2]{1,2,0:T(2,128)S(1)} %copy.14), channel_id=1, source_target_pairs={{4,0},{8,4},{12,8},{16,12},{20,16},{24,20},{28,24},{0,28},{5,1},{9... | collective-permute-start | bytes 43688 | tf_op jit(solution)/shard_map/ppermute | solution.py:19
  66.9 0.4 copy.13
  67.3 0.5 collective-permute-done.3
  67.8 0.4 copy.16
  68.1 4.5 %collective-permute-done.2 = f32[7,260,2]{1,2,0:T(2,128)S(1)} collective-permute-done((f32[7,260,2]{1,2,0:T(2,128)S(1)}, f32[7,260,2]{1,2,0:T(2,128)S(1)}, u32[]{:S(2)}, u32[]{:S(2)}) %collective-permute-start.2) | collective-permute-done | bytes 14592 | tf_op jit(solution)/shard_map/ppermute | solution.py:16
  72.7 1.3 copy.15
  74.0 1.6 maximum_bitcast_fusion
  75.5 0.4 multiply_add_fusion.1
  75.9 0.5 multiply_add_fusion
  76.4 0.3 copy-done
  76.7 0.4 maximum_bitcast_fusion.3
  77.1 0.2 broadcast_compare_fusion.1
  77.5 0.2 slice_multiply_fusion.1
  77.8 0.3 broadcast_compare_fusion
  78.0 0.3 slice_multiply_fusion
  78.6 1.0 pad_maximum_fusion
  79.7 1.3 fusion.23
  81.1 0.9 fusion.55
  82.1 0.2 fusion.61
  82.3 24.0 %all-gather.1 = f32[16,2,256]{2,1,0:T(2,128)S(1)} all-gather(f32[2,2,256]{2,1,0:T(2,128)S(1)} %get-tuple-element.53), channel_id=3, replica_groups=mesh['lon'=8,'lat'=4] {'lon'}, dimensions={0}, use_global_device_ids=true | all-gather | bytes 36864 | tf_op jit(solution)/shard_map/all_gather | solution.py:139
  106.4 16.3 %collective-permute-start.4 = (f32[2,2,256]{2,1,0:T(2,128)S(1)}, f32[2,2,256]{2,1,0:T(2,128)S(1)}, u32[]{:S(2)}, u32[]{:S(2)}) collective-permute-start(f32[2,2,256]{2,1,0:T(2,128)S(1)} %get-tuple-element.53), channel_id=1, source_target_pairs={{0,1},{1,2},{2,3},{4,5},{5,6},{6,7},{8,9},{9,10},{10,11},{12,13},{... | collective-permute-start | bytes 12296 | tf_op jit(solution)/shard_map/ppermute | solution.py:16
  122.8 1.9 collective-permute-start.5
  124.7 0.2 rev.13
  124.9 2.8 %collective-permute-done.5 = f32[2,2,256]{2,1,0:T(2,128)S(1)} collective-permute-done((f32[2,2,256]{2,1,0:T(2,128)S(1)}, f32[2,2,256]{2,1,0:T(2,128)S(1)}, u32[]{:S(2)}, u32[]{:S(2)}) %collective-permute-start.5) | collective-permute-done | bytes 4128 | tf_op jit(solution)/shard_map/ppermute | solution.py:19
  128.0 1.5 collective-permute-start.7
  129.4 11.1 %collective-permute-done.6 = f32[2,260,2]{2,1,0:T(8,128)S(1)} collective-permute-done((f32[2,260,2]{2,1,0:T(8,128)S(1)}, f32[2,260,2]{2,1,0:T(8,128)S(1)}, u32[]{:S(2)}, u32[]{:S(2)}) %collective-permute-start.6) | collective-permute-done | bytes 4192 | tf_op jit(solution)/shard_map/ppermute | solution.py:19
  140.6 0.3 pad_maximum_fusion.2
  141.0 1.3 fusion.17
  142.4 0.9 fusion.47
  143.3 0.2 fusion.60
  143.6 24.0 %all-gather.2 = f32[16,2,256]{2,1,0:T(2,128)S(1)} all-gather(f32[2,2,256]{2,1,0:T(2,128)S(1)} %get-tuple-element.51), channel_id=4, replica_groups=mesh['lon'=8,'lat'=4] {'lon'}, dimensions={0}, use_global_device_ids=true | all-gather | bytes 36864 | tf_op jit(solution)/shard_map/all_gather | solution.py:139
  167.6 8.1 %collective-permute-start.8 = (f32[2,2,256]{2,1,0:T(2,128)S(1)}, f32[2,2,256]{2,1,0:T(2,128)S(1)}, u32[]{:S(2)}, u32[]{:S(2)}) collective-permute-start(f32[2,2,256]{2,1,0:T(2,128)S(1)} %get-tuple-element.51), channel_id=1, source_target_pairs={{0,1},{1,2},{2,3},{4,5},{5,6},{6,7},{8,9},{9,10},{10,11},{12,13},{... | collective-permute-start | bytes 12296 | tf_op jit(solution)/shard_map/ppermute | solution.py:16
  175.8 1.9 collective-permute-start.9
  177.7 0.2 rev.14
  177.9 2.8 %collective-permute-done.9 = f32[2,2,256]{2,1,0:T(2,128)S(1)} collective-permute-done((f32[2,2,256]{2,1,0:T(2,128)S(1)}, f32[2,2,256]{2,1,0:T(2,128)S(1)}, u32[]{:S(2)}, u32[]{:S(2)}) %collective-permute-start.9) | collective-permute-done | bytes 4128 | tf_op jit(solution)/shard_map/ppermute | solution.py:19
  180.9 1.5 collective-permute-start.10
  182.5 11.1 %collective-permute-done.10 = f32[2,260,2]{2,1,0:T(8,128)S(1)} collective-permute-done((f32[2,260,2]{2,1,0:T(8,128)S(1)}, f32[2,260,2]{2,1,0:T(8,128)S(1)}, u32[]{:S(2)}, u32[]{:S(2)}) %collective-permute-start.10) | collective-permute-done | bytes 4192 | tf_op jit(solution)/shard_map/ppermute | solution.py:19
  193.6 0.3 pad_maximum_fusion.3
  194.0 1.3 fusion.11
  195.4 0.9 fusion.39
  196.3 0.2 fusion.59
  196.6 24.0 %all-gather.3 = f32[16,2,256]{2,1,0:T(2,128)S(1)} all-gather(f32[2,2,256]{2,1,0:T(2,128)S(1)} %get-tuple-element.49), channel_id=5, replica_groups=mesh['lon'=8,'lat'=4] {'lon'}, dimensions={0}, use_global_device_ids=true | all-gather | bytes 36864 | tf_op jit(solution)/shard_map/all_gather | solution.py:139
  220.6 8.2 %collective-permute-start.12 = (f32[2,2,256]{2,1,0:T(2,128)S(1)}, f32[2,2,256]{2,1,0:T(2,128)S(1)}, u32[]{:S(2)}, u32[]{:S(2)}) collective-permute-start(f32[2,2,256]{2,1,0:T(2,128)S(1)} %get-tuple-element.49), channel_id=1, source_target_pairs={{0,1},{1,2},{2,3},{4,5},{5,6},{6,7},{8,9},{9,10},{10,11},{12,13},{... | collective-permute-start | bytes 12296 | tf_op jit(solution)/shard_map/ppermute | solution.py:16
  228.8 1.9 collective-permute-start.13
  230.7 0.2 rev.15
  231.0 2.8 %collective-permute-done.13 = f32[2,2,256]{2,1,0:T(2,128)S(1)} collective-permute-done((f32[2,2,256]{2,1,0:T(2,128)S(1)}, f32[2,2,256]{2,1,0:T(2,128)S(1)}, u32[]{:S(2)}, u32[]{:S(2)}) %collective-permute-start.13) | collective-permute-done | bytes 4128 | tf_op jit(solution)/shard_map/ppermute | solution.py:19
  233.9 1.6 collective-permute-start.14
  235.5 11.1 %collective-permute-done.14 = f32[2,260,2]{2,1,0:T(8,128)S(1)} collective-permute-done((f32[2,260,2]{2,1,0:T(8,128)S(1)}, f32[2,260,2]{2,1,0:T(8,128)S(1)}, u32[]{:S(2)}, u32[]{:S(2)}) %collective-permute-start.14) | collective-permute-done | bytes 4192 | tf_op jit(solution)/shard_map/ppermute | solution.py:19
  246.6 0.3 pad_maximum_fusion.4
  247.0 1.3 fusion.5
  248.4 0.9 fusion.31
  249.3 0.2 fusion.58
  249.6 0.8 slice_bitcast_fusion
  (137 shorter events, 1.8 us)
Async XLA Ops:
  0.6 27.5 %copy-start.48 = (f32[256,256]{1,0:T(8,128)S(1)}, f32[256,256]{1,0:T(8,128)}, u32[]{:S(2)}) copy-start(f32[256,256]{1,0:T(8,128)} %param.16) | copy-start | bytes 786436
  5.6 22.6 %copy-start.49 = (f32[256,256]{1,0:T(8,128)S(1)}, f32[256,256]{1,0:T(8,128)}, u32[]{:S(2)}) copy-start(f32[256,256]{1,0:T(8,128)} %param.17) | copy-start | bytes 786436
  5.6 22.6 %copy-start.40 = (f32[256,256]{1,0:T(8,128)S(1)}, f32[256,256]{1,0:T(8,128)}, u32[]{:S(2)}) copy-start(f32[256,256]{1,0:T(8,128)} %param.11) | copy-start | bytes 786436
  5.6 22.7 %copy-start.42 = (f32[256,256]{1,0:T(8,128)S(1)}, f32[256,256]{1,0:T(8,128)}, u32[]{:S(2)}) copy-start(f32[256,256]{1,0:T(8,128)} %param.12) | copy-start | bytes 786436
  17.7 42.1 %copy-start.50 = (f32[7]{0:T(128)S(1)}, f32[7]{0:T(128)}, u32[]{:S(2)}) copy-start(f32[7]{0:T(128)} %constant.24.clone) | copy-start | bytes 88
  28.3 31.5 %collective-permute-start.1 = (f32[7,2,256]{2,1,0:T(2,128)S(1)}, f32[7,2,256]{2,1,0:T(2,128)S(1)}, u32[]{:S(2)}, u32[]{:S(2)}) collective-permute-start(f32[7,2,256]{2,1,0:T(2,128)S(1)} %get-tuple-element.33), channel_id=1, source_target_pairs={{1,0},{2,1},{3,2},{5,4},{6,5},{7,6},{9,8},{10,9},{11,10},{13,12},{... | collective-permute-start | bytes 43016 | tf_op jit(solution)/shard_map/ppermute | solution.py:19
  30.3 29.6 %collective-permute-start = (f32[7,2,256]{2,1,0:T(2,128)S(1)}, f32[7,2,256]{2,1,0:T(2,128)S(1)}, u32[]{:S(2)}, u32[]{:S(2)}) collective-permute-start(f32[7,2,256]{2,1,0:T(2,128)S(1)} %get-tuple-element.32), channel_id=1, source_target_pairs={{0,1},{1,2},{2,3},{4,5},{5,6},{6,7},{8,9},{9,10},{10,11},{12,13},{... | collective-permute-start | bytes 43016 | tf_op jit(solution)/shard_map/ppermute | solution.py:16
  59.9 16.5 %copy-start.44 = (f32[7,2,256]{2,1,0:T(2,128)}, f32[7,2,256]{2,1,0:T(2,128)S(1)}, u32[]{:S(2)}) copy-start(f32[7,2,256]{2,1,0:T(2,128)S(1)} %multiply_select_fusion) | copy-start | bytes 43012
  59.9 16.5 %copy-start.46 = (f32[7,2,256]{2,1,0:T(2,128)}, f32[7,2,256]{2,1,0:T(2,128)S(1)}, u32[]{:S(2)}) copy-start(f32[7,2,256]{2,1,0:T(2,128)S(1)} %collective-permute-done) | copy-start | bytes 43012
  62.9 4.9 %collective-permute-start.3 = (f32[7,260,2]{1,2,0:T(2,128)S(1)}, f32[7,260,2]{1,2,0:T(2,128)S(1)}, u32[]{:S(2)}, u32[]{:S(2)}) collective-permute-start(f32[7,260,2]{1,2,0:T(2,128)S(1)} %copy.14), channel_id=1, source_target_pairs={{4,0},{8,4},{12,8},{16,12},{20,16},{24,20},{28,24},{0,28},{5,1},{9... | collective-permute-start | bytes 43688 | tf_op jit(solution)/shard_map/ppermute | solution.py:19
  67.3 5.4 %collective-permute-start.2 = (f32[7,260,2]{1,2,0:T(2,128)S(1)}, f32[7,260,2]{1,2,0:T(2,128)S(1)}, u32[]{:S(2)}, u32[]{:S(2)}) collective-permute-start(f32[7,260,2]{1,2,0:T(2,128)S(1)} %copy.13), channel_id=1, source_target_pairs={{0,4},{4,8},{8,12},{12,16},{16,20},{20,24},{24,28},{28,0},{1,5},{5... | collective-permute-start | bytes 43688 | tf_op jit(solution)/shard_map/ppermute | solution.py:16
  75.5 1.2 copy-start
  75.9 5.1 %copy-start.18 = (f32[257,256]{1,0:T(8,128)}, f32[257,256]{1,0:T(8,128)S(1)}, u32[]{:S(2)}) copy-start(f32[257,256]{1,0:T(8,128)S(1)} %get-tuple-element.56) | copy-start | bytes 789508
  75.9 5.1 %copy-start.22 = (f32[257,256]{1,0:T(8,128)}, f32[257,256]{1,0:T(8,128)S(1)}, u32[]{:S(2)}) copy-start(f32[257,256]{1,0:T(8,128)S(1)} %get-tuple-element.57) | copy-start | bytes 789508
  76.7 2.9 %copy-start.1 = (f32[256,257]{1,0:T(8,128)}, f32[256,257]{1,0:T(8,128)S(1)}, u32[]{:S(2)}) copy-start(f32[256,257]{1,0:T(8,128)S(1)} %get-tuple-element.54) | copy-start | bytes 789508
  76.7 2.9 %copy-start.4 = (f32[256,257]{1,0:T(8,128)}, f32[256,257]{1,0:T(8,128)S(1)}, u32[]{:S(2)}) copy-start(f32[256,257]{1,0:T(8,128)S(1)} %get-tuple-element.55) | copy-start | bytes 789508
  77.3 3.7 %copy-start.38 = (pred[257,256]{1,0:T(8,128)(4,1)}, pred[257,256]{1,0:T(8,128)(4,1)S(1)}, u32[]{:S(2)}) copy-start(pred[257,256]{1,0:T(8,128)(4,1)S(1)} %get-tuple-element.4) | copy-start | bytes 197380
  77.3 65.0 %copy-start.15 = (f32[257,256]{1,0:T(8,128)}, f32[257,256]{1,0:T(8,128)S(1)}, u32[]{:S(2)}) copy-start(f32[257,256]{1,0:T(8,128)S(1)} %get-tuple-element.5) | copy-start | bytes 789508
  77.5 4.5 %copy-start.34 = (f32[256,256]{1,0:T(8,128)}, f32[256,256]{1,0:T(8,128)S(1)}, u32[]{:S(2)}) copy-start(f32[256,256]{1,0:T(8,128)S(1)} %slice.772) | copy-start | bytes 786436
  77.7 3.3 %copy-start.26 = (f32[257,256]{1,0:T(8,128)}, f32[257,256]{1,0:T(8,128)S(1)}, u32[]{:S(2)}) copy-start(f32[257,256]{1,0:T(8,128)S(1)} %get-tuple-element.90) | copy-start | bytes 789508
  77.7 3.3 %copy-start.30 = (f32[257,256]{1,0:T(8,128)}, f32[257,256]{1,0:T(8,128)S(1)}, u32[]{:S(2)}) copy-start(f32[257,256]{1,0:T(8,128)S(1)} %get-tuple-element.91) | copy-start | bytes 789508
  78.6 1.1 copy-start.7
  78.6 1.1 copy-start.11
  81.1 1.0 copy-start.41
  81.1 1.0 copy-start.43
  106.4 21.3 %collective-permute-start.4 = (f32[2,2,256]{2,1,0:T(2,128)S(1)}, f32[2,2,256]{2,1,0:T(2,128)S(1)}, u32[]{:S(2)}, u32[]{:S(2)}) collective-permute-start(f32[2,2,256]{2,1,0:T(2,128)S(1)} %get-tuple-element.53), channel_id=1, source_target_pairs={{0,1},{1,2},{2,3},{4,5},{5,6},{6,7},{8,9},{9,10},{10,11},{12,13},{... | collective-permute-start | bytes 12296 | tf_op jit(solution)/shard_map/ppermute | solution.py:16
  122.8 4.9 %collective-permute-start.5 = (f32[2,2,256]{2,1,0:T(2,128)S(1)}, f32[2,2,256]{2,1,0:T(2,128)S(1)}, u32[]{:S(2)}, u32[]{:S(2)}) collective-permute-start(f32[2,2,256]{2,1,0:T(2,128)S(1)} %get-tuple-element.52), channel_id=1, source_target_pairs={{1,0},{2,1},{3,2},{5,4},{6,5},{7,6},{9,8},{10,9},{11,10},{13,12},{... | collective-permute-start | bytes 12296 | tf_op jit(solution)/shard_map/ppermute | solution.py:19
  127.7 13.2 %copy-start.2 = (f32[256,257]{1,0:T(8,128)S(1)}, f32[256,257]{1,0:T(8,128)}, u32[]{:S(2)}) copy-start(f32[256,257]{1,0:T(8,128)} %copy-done.1) | copy-start | bytes 789508
  127.8 13.2 %copy-start.5 = (f32[256,257]{1,0:T(8,128)S(1)}, f32[256,257]{1,0:T(8,128)}, u32[]{:S(2)}) copy-start(f32[256,257]{1,0:T(8,128)} %copy-done.4) | copy-start | bytes 789508
  127.8 13.2 %copy-start.8 = (f32[256,257]{1,0:T(8,128)S(1)}, f32[256,257]{1,0:T(8,128)}, u32[]{:S(2)}) copy-start(f32[256,257]{1,0:T(8,128)} %copy-done.7) | copy-start | bytes 789508
  127.8 13.2 %copy-start.12 = (f32[256,257]{1,0:T(8,128)S(1)}, f32[256,257]{1,0:T(8,128)}, u32[]{:S(2)}) copy-start(f32[256,257]{1,0:T(8,128)} %copy-done.11) | copy-start | bytes 789508
  127.9 12.7 %collective-permute-start.6 = (f32[2,260,2]{2,1,0:T(8,128)S(1)}, f32[2,260,2]{2,1,0:T(8,128)S(1)}, u32[]{:S(2)}, u32[]{:S(2)}) collective-permute-start(f32[2,260,2]{2,1,0:T(8,128)S(1)} %get-tuple-element.38), channel_id=1, source_target_pairs={{4,0},{8,4},{12,8},{16,12},{20,16},{24,20},{28,24},{0,28},{5,1},{9... | collective-permute-start | bytes 12488 | tf_op jit(solution)/shard_map/ppermute | solution.py:19
  128.0 12.6 %collective-permute-start.7 = (f32[2,260,2]{2,1,0:T(8,128)S(1)}, f32[2,260,2]{2,1,0:T(8,128)S(1)}, u32[]{:S(2)}, u32[]{:S(2)}) collective-permute-start(f32[2,260,2]{2,1,0:T(8,128)S(1)} %get-tuple-element.39), channel_id=1, source_target_pairs={{0,4},{4,8},{8,12},{12,16},{16,20},{20,24},{24,28},{28,0},{1,5},{5... | collective-permute-start | bytes 12488 | tf_op jit(solution)/shard_map/ppermute | solution.py:16
  140.9 1.4 copy-start.19
  140.9 1.4 copy-start.23
  141.0 1.4 copy-start.27
  141.0 1.4 copy-start.31
  141.0 1.4 copy-start.39
  142.4 1.0 copy-start.35
  167.6 13.1 %collective-permute-start.8 = (f32[2,2,256]{2,1,0:T(2,128)S(1)}, f32[2,2,256]{2,1,0:T(2,128)S(1)}, u32[]{:S(2)}, u32[]{:S(2)}) collective-permute-start(f32[2,2,256]{2,1,0:T(2,128)S(1)} %get-tuple-element.51), channel_id=1, source_target_pairs={{0,1},{1,2},{2,3},{4,5},{5,6},{6,7},{8,9},{9,10},{10,11},{12,13},{... | collective-permute-start | bytes 12296 | tf_op jit(solution)/shard_map/ppermute | solution.py:16
  175.8 4.9 %collective-permute-start.9 = (f32[2,2,256]{2,1,0:T(2,128)S(1)}, f32[2,2,256]{2,1,0:T(2,128)S(1)}, u32[]{:S(2)}, u32[]{:S(2)}) collective-permute-start(f32[2,2,256]{2,1,0:T(2,128)S(1)} %get-tuple-element.50), channel_id=1, source_target_pairs={{1,0},{2,1},{3,2},{5,4},{6,5},{7,6},{9,8},{10,9},{11,10},{13,12},{... | collective-permute-start | bytes 12296 | tf_op jit(solution)/shard_map/ppermute | solution.py:19
  180.8 13.2 %copy-start.3 = (f32[256,257]{1,0:T(8,128)S(1)}, f32[256,257]{1,0:T(8,128)}, u32[]{:S(2)}) copy-start(f32[256,257]{1,0:T(8,128)} %copy-done.1) | copy-start | bytes 789508
  180.8 13.2 %copy-start.6 = (f32[256,257]{1,0:T(8,128)S(1)}, f32[256,257]{1,0:T(8,128)}, u32[]{:S(2)}) copy-start(f32[256,257]{1,0:T(8,128)} %copy-done.4) | copy-start | bytes 789508
  180.8 13.2 %copy-start.9 = (f32[256,257]{1,0:T(8,128)S(1)}, f32[256,257]{1,0:T(8,128)}, u32[]{:S(2)}) copy-start(f32[256,257]{1,0:T(8,128)} %copy-done.7) | copy-start | bytes 789508
  180.8 13.2 %copy-start.13 = (f32[256,257]{1,0:T(8,128)S(1)}, f32[256,257]{1,0:T(8,128)}, u32[]{:S(2)}) copy-start(f32[256,257]{1,0:T(8,128)} %copy-done.11) | copy-start | bytes 789508
  180.9 12.7 %collective-permute-start.10 = (f32[2,260,2]{2,1,0:T(8,128)S(1)}, f32[2,260,2]{2,1,0:T(8,128)S(1)}, u32[]{:S(2)}, u32[]{:S(2)}) collective-permute-start(f32[2,260,2]{2,1,0:T(8,128)S(1)} %get-tuple-element.36), channel_id=1, source_target_pairs={{4,0},{8,4},{12,8},{16,12},{20,16},{24,20},{28,24},{0,28},{5,1},{9... | collective-permute-start | bytes 12488 | tf_op jit(solution)/shard_map/ppermute | solution.py:19
  182.5 11.2 %collective-permute-start.11 = (f32[2,260,2]{2,1,0:T(8,128)S(1)}, f32[2,260,2]{2,1,0:T(8,128)S(1)}, u32[]{:S(2)}, u32[]{:S(2)}) collective-permute-start(f32[2,260,2]{2,1,0:T(8,128)S(1)} %get-tuple-element.37), channel_id=1, source_target_pairs={{0,4},{4,8},{8,12},{12,16},{16,20},{20,24},{24,28},{28,0},{1,5},{5... | collective-permute-start | bytes 12488 | tf_op jit(solution)/shard_map/ppermute | solution.py:16
  194.0 1.4 copy-start.16
  194.0 1.4 copy-start.20
  194.0 1.4 copy-start.24
  194.0 1.4 copy-start.28
  194.0 1.4 copy-start.32
  195.4 1.0 copy-start.36
  220.6 13.1 %collective-permute-start.12 = (f32[2,2,256]{2,1,0:T(2,128)S(1)}, f32[2,2,256]{2,1,0:T(2,128)S(1)}, u32[]{:S(2)}, u32[]{:S(2)}) collective-permute-start(f32[2,2,256]{2,1,0:T(2,128)S(1)} %get-tuple-element.49), channel_id=1, source_target_pairs={{0,1},{1,2},{2,3},{4,5},{5,6},{6,7},{8,9},{9,10},{10,11},{12,13},{... | collective-permute-start | bytes 12296 | tf_op jit(solution)/shard_map/ppermute | solution.py:16
  228.8 4.9 %collective-permute-start.13 = (f32[2,2,256]{2,1,0:T(2,128)S(1)}, f32[2,2,256]{2,1,0:T(2,128)S(1)}, u32[]{:S(2)}, u32[]{:S(2)}) collective-permute-start(f32[2,2,256]{2,1,0:T(2,128)S(1)} %get-tuple-element.48), channel_id=1, source_target_pairs={{1,0},{2,1},{3,2},{5,4},{6,5},{7,6},{9,8},{10,9},{11,10},{13,12},{... | collective-permute-start | bytes 12296 | tf_op jit(solution)/shard_map/ppermute | solution.py:19
  233.8 13.1 %copy-start.10 = (f32[256,257]{1,0:T(8,128)S(1)}, f32[256,257]{1,0:T(8,128)}, u32[]{:S(2)}) copy-start(f32[256,257]{1,0:T(8,128)} %copy-done.7) | copy-start | bytes 789508
  233.8 13.1 %copy-start.14 = (f32[256,257]{1,0:T(8,128)S(1)}, f32[256,257]{1,0:T(8,128)}, u32[]{:S(2)}) copy-start(f32[256,257]{1,0:T(8,128)} %copy-done.11) | copy-start | bytes 789508
  233.9 12.7 %collective-permute-start.14 = (f32[2,260,2]{2,1,0:T(8,128)S(1)}, f32[2,260,2]{2,1,0:T(8,128)S(1)}, u32[]{:S(2)}, u32[]{:S(2)}) collective-permute-start(f32[2,260,2]{2,1,0:T(8,128)S(1)} %get-tuple-element.34), channel_id=1, source_target_pairs={{4,0},{8,4},{12,8},{16,12},{20,16},{24,20},{28,24},{0,28},{5,1},{9... | collective-permute-start | bytes 12488 | tf_op jit(solution)/shard_map/ppermute | solution.py:19
  235.5 11.1 %collective-permute-start.15 = (f32[2,260,2]{2,1,0:T(8,128)S(1)}, f32[2,260,2]{2,1,0:T(8,128)S(1)}, u32[]{:S(2)}, u32[]{:S(2)}) collective-permute-start(f32[2,260,2]{2,1,0:T(8,128)S(1)} %get-tuple-element.35), channel_id=1, source_target_pairs={{0,4},{4,8},{8,12},{12,16},{16,20},{20,24},{24,28},{28,0},{1,5},{5... | collective-permute-start | bytes 12488 | tf_op jit(solution)/shard_map/ppermute | solution.py:16
  246.9 1.4 copy-start.17
  247.0 1.4 copy-start.21
  247.0 1.4 copy-start.25
  247.0 1.4 copy-start.29
  247.0 1.4 copy-start.33
  (3 other events, 2.5 us)
where the time goes:
time: 251 us; the launch traced here: 250 us
  blocking collectives  96.9 us (39%)
  starting transfers between devices  53.4 us (21%)
  waiting for transfers between devices  46.7 us (19%)
  other arithmetic  39.4 us (16%)
  local copies, waits for them, and re-layouts  12.2 us (5%)
    all_gather x4, blocking collectives, mirror_rows(): every = lax.all_gather(top_rows[None], 'lon', axis=0, tiled=True)  96.9 us
    ppermute x8, waiting for transfers between devices, padded(): lax.ppermute(lax.slice_in_dim(block, 0, width, axis=dim), axis, backward)  42.1 us
    ppermute x8, starting transfers between devices, padded(): lax.ppermute(lax.slice_in_dim(block, block.shape[dim] - width, None, axis...  38.6 us
    unnamed x3, other arithmetic  23.5 us
    ppermute x8, starting transfers between devices, padded(): lax.ppermute(lax.slice_in_dim(block, 0, width, axis=dim), axis, backward)  14.8 us
    mul x10, other arithmetic, face_flux_terms(): lower_mask * upper_mask  9.37 us
  transfers between devices with their start and end apart: 16, of which 8 were waited for; matrix products, arithmetic and copies ran while one was open for 1% of the time, Pallas kernels for 0%

commit v1 on v0

v1 whole, which is shorter than its diff:
```python
import functools

import jax
import jax.numpy as jnp
from jax import lax
from jax.experimental import pallas as pl
from jax.experimental.pallas import tpu as pltpu
from jax.sharding import PartitionSpec as P

STEPS = 4
HALO = 2 * STEPS
FIELDS = 6
LANES = 128
PAD = 8
BASE = PAD + HALO
PACKED = FIELDS * HALO
HALF = 64
MESH = pl.DeviceIdType.MESH


def lane_index(rows=8):
    return lax.broadcasted_iota(jnp.int32, (rows, LANES), 1)


def kernel(
    nlat, nlon,
    t_in, s_in, m_in, k_in, table, u_in, v_in,
    t_out, s_out,
    ext, qb, ints, slope, coef, gy,
    pack, pack_t, tops, bots,
    col_t, nbuf, sbuf, corner, comb,
    load_sem, send_sem, recv_sem,
):
    rows, cols = t_in.shape
    own = cols // LANES
    nt = own + 1
    lat = lax.axis_index("lat")
    lon = lax.axis_index("lon")
    top = lat == nlat - 1
    low = lat == 0
    east = lax.rem(lon + 1, nlon)
    west = lax.rem(lon + nlon - 1, nlon)
    fold = nlon - 1 - lon
    fold_e = lax.rem(2 * nlon - 2 - lon, nlon)
    fold_w = lax.rem(nlon - lon, nlon)

    loads = []
    for f, ref in enumerate((t_in, s_in, u_in, v_in)):
        for t in range(own):
            loads.append(pltpu.make_async_copy(
                ref.at[:, pl.ds(LANES * t, LANES)],
                ext.at[f, t, pl.ds(BASE, rows), :],
                load_sem.at[len(loads)]))
    for f, ref in enumerate((m_in, k_in)):
        for t in range(own):
            loads.append(pltpu.make_async_copy(
                ref.at[:, pl.ds(LANES * t, LANES)],
                ints.at[f, t],
                load_sem.at[len(loads)]))
    for c in loads:
        c.start()

    barrier = pltpu.get_barrier_semaphore()

    def greet(a, o):
        pl.semaphore_signal(barrier, inc=1, device_id=(o, a), device_id_type=MESH)

    greet(lat, east)
    greet(lat, west)

    @pl.when(jnp.logical_not(top))
    def _():
        greet(lat + 1, lon)
        greet(lat + 1, east)
        greet(lat + 1, west)

    @pl.when(jnp.logical_not(low))
    def _():
        greet(lat - 1, lon)
        greet(lat - 1, east)
        greet(lat - 1, west)

    @pl.when(top)
    def _():
        greet(lat, fold)

        @pl.when(fold_e != lon)
        def _():
            greet(lat, fold_e)

        @pl.when(fold_w != lon)
        def _():
            greet(lat, fold_w)

    for c in loads:
        c.wait()

    lane = lane_index()

    def pack_rows(i, _):
        r = pl.multiple_of(i * 8, 8)
        out = jnp.zeros((8, LANES), jnp.float32)
        for f in range(FIELDS):
            if f < 4:
                first = ext[f, 0, pl.ds(BASE + r, 8), :]
                last = ext[f, own - 1, pl.ds(BASE + r, 8), :]
            else:
                parts = [ints[f - 4, t, pl.ds(r, 8), :].astype(jnp.float32) for t in range(own)]
                for t in range(own):
                    ext[f, t, pl.ds(BASE + r, 8), :] = parts[t]
                first, last = parts[0], parts[-1]
            a = HALO * f
            b = HALF + HALO * f
            out = jnp.where((lane >= a) & (lane < a + HALO),
                            pltpu.roll(first, a, 1) if a else first, out)
            out = jnp.where((lane >= b) & (lane < b + HALO),
                            pltpu.roll(last, (b - (LANES - HALO)) % LANES, 1), out)
        pack[pl.ds(r, 8), :] = out
        return 0

    lax.fori_loop(0, rows // 8, pack_rows, 0)
    for h in range(rows // LANES):
        pack_t[:, pl.ds(LANES * h, LANES)] = pack[pl.ds(LANES * h, LANES), :].T
    for f in range(FIELDS):
        for t in range(own):
            tops[pl.ds(8 * f, 8), pl.ds(LANES * t, LANES)] = ext[f, t, pl.ds(BASE + rows - 8, 8), :]
            bots[pl.ds(8 * f, 8), pl.ds(LANES * t, LANES)] = ext[f, t, pl.ds(BASE, 8), :]

    others = lambda x: jnp.where(x, 1, 0)
    count = 2 + 3 * others(jnp.logical_not(low)) + others(top) * (
        1 + others(fold_e != lon) + others(fold_w != lon)) + 3 * others(jnp.logical_not(top))
    pl.semaphore_wait(barrier, count)

    pack_top = pack.at[pl.ds(rows - 8, 8), :]
    pack_low = pack.at[pl.ds(0, 8), :]
    from_west = col_t.at[pl.ds(HALF, PACKED), :]
    from_east = col_t.at[pl.ds(0, PACKED), :]

    def rdma(src, dst, s, r, a, o):
        return pltpu.make_async_remote_copy(
            src_ref=src, dst_ref=dst, send_sem=send_sem.at[s], recv_sem=recv_sem.at[r],
            device_id=(o, a), device_id_type=MESH)

    to_east = rdma(pack_t.at[pl.ds(HALF, PACKED), :], from_west, 0, 0, lat, east)
    to_west = rdma(pack_t.at[pl.ds(0, PACKED), :], from_east, 1, 1, lat, west)
    north = [
        rdma(tops, sbuf, 2, 3, lat + 1, lon),
        rdma(pack_top, corner.at[1], 3, 5, lat + 1, east),
        rdma(pack_top, corner.at[0], 4, 4, lat + 1, west),
    ]
    mirror = rdma(tops, nbuf, 2, 2, lat, fold)
    mirror_e = rdma(pack_top, corner.at[2], 3, 6, lat, fold_e)
    mirror_w = rdma(pack_top, corner.at[3], 4, 7, lat, fold_w)
    south = [
        rdma(bots, nbuf, 5, 2, lat - 1, lon),
        rdma(pack_low, corner.at[3], 6, 7, lat - 1, east),
        rdma(pack_low, corner.at[2], 7, 6, lat - 1, west),
    ]

    to_east.start()
    to_west.start()

    @pl.when(top)
    def _():
        mirror.start()

        @pl.when(fold_e != lon)
        def _():
            mirror_e.start()

        @pl.when(fold_w != lon)
        def _():
            mirror_w.start()

        @pl.when(fold_e == lon)
        def _():
            corner[2] = pack[pl.ds(rows - 8, 8), :]

        @pl.when(fold_w == lon)
        def _():
            corner[3] = pack[pl.ds(rows - 8, 8), :]

    @pl.when(jnp.logical_not(top))
    def _():
        for c in north:
            c.start()

    @pl.when(jnp.logical_not(low))
    def _():
        for c in south:
            c.start()

    nclass = table.shape[0]

    def slopes(idx):
        res = []
        for d in range(2):
            vals = [table[k, d] for k in range(nclass)]
            bit = 1
            while len(vals) > 1:
                on = (idx & bit) != 0
                vals = [jnp.where(on, vals[j + 1], vals[j]) if j + 1 < len(vals) else vals[j]
                        for j in range(0, len(vals), 2)]
                bit *= 2
            res.append(vals[0])
        return res

    def own_slopes(i, _):
        r = pl.multiple_of(i * 8, 8)
        for t in range(own):
            a, b = slopes(ints[1, t, pl.ds(r, 8), :])
            slope[0, t, pl.ds(BASE + r, 8), :] = a
            slope[1, t, pl.ds(BASE + r, 8), :] = b
        return 0

    lax.fori_loop(0, rows // 8, own_slopes, 0)

    to_east.wait_recv()
    to_west.wait_recv()
    for h in range(rows // LANES):
        comb[pl.ds(HALO + LANES * h, LANES), :] = col_t[:, pl.ds(LANES * h, LANES)].T

    @pl.when(low)
    def _():
        comb[pl.ds(0, 8), :] = jnp.zeros((8, LANES), jnp.float32)
        for f in range(FIELDS):
            for t in range(own):
                ext[f, t, pl.ds(PAD, 8), :] = jnp.zeros((8, LANES), jnp.float32)

    @pl.when(jnp.logical_not(low))
    def _():
        north[0].wait_recv()
        north[1].wait_recv()
        north[2].wait_recv()
        comb[pl.ds(0, 8), :] = jnp.where(lane < HALF, corner[0], corner[1])
        for f in range(FIELDS):
            for t in range(own):
                ext[f, t, pl.ds(PAD, 8), :] = sbuf[pl.ds(8 * f, 8), pl.ds(LANES * t, LANES)]

    mirror.wait_recv()

    @pl.when(jnp.logical_not(top))
    def _():
        mirror_e.wait_recv()
        mirror_w.wait_recv()
        comb[pl.ds(HALO + rows, 8), :] = jnp.where(lane < HALF, corner[2], corner[3])
        for f in range(FIELDS):
            for t in range(own):
                ext[f, t, pl.ds(BASE + rows, 8), :] = nbuf[pl.ds(8 * f, 8), pl.ds(LANES * t, LANES)]

    @pl.when(top)
    def _():
        @pl.when(fold_e != lon)
        def _():
            mirror_e.wait_recv()

        @pl.when(fold_w != lon)
        def _():
            mirror_w.wait_recv()

        def dot(a, b):
            return jnp.dot(a, b, precision=lax.Precision.HIGHEST, preferred_element_type=jnp.float32)

        def iotas(n):
            return (lax.broadcasted_iota(jnp.int32, (n, n), 0), lax.broadcasted_iota(jnp.int32, (n, n), 1))

        i, j = iotas(cols)
        flip = jnp.where(i + j == cols - 1, 1.0, 0.0)
        i, j = iotas(PACKED)
        turn = jnp.where(j == i + 7 - 2 * (i & 7), 1.0, 0.0)
        turned = dot(turn, dot(nbuf[...], flip))
        for f in range(FIELDS):
            sign = -1.0 if f in (2, 3) else 1.0
            for t in range(own):
                ext[f, t, pl.ds(BASE + rows, 8), :] = sign * turned[8 * f:8 * f + 8, LANES * t:LANES * t + LANES]
        i, j = iotas(LANES)
        swap = jnp.where(i == ((j + HALF) & 127) + 7 - 2 * (j & 7), 1.0, 0.0)
        i, j = iotas(8)
        turn8 = jnp.where(i + j == 7, 1.0, 0.0)
        mixed = jnp.where(lane >= HALF, corner[2], corner[3])
        mixed = dot(turn8, dot(mixed, swap))
        flipped = ((lane & 63) >= 2 * HALO) & ((lane & 63) < 4 * HALO)
        comb[pl.ds(HALO + rows, 8), :] = jnp.where(flipped, -mixed, mixed)

    def unpack(i, _):
        r = pl.multiple_of(i * 8, 8)
        both = comb[pl.ds(r, 8), :]
        for f in range(FIELDS):
            a = pltpu.roll(both, (-HALO * f) % LANES, 1) if f else both
            b = pltpu.roll(both, (LANES - HALO - HALF - HALO * f) % LANES, 1)
            third = jnp.where(lane < HALF, a, b)
            if f < 5:
                ext[f, own, pl.ds(PAD + r, 8), :] = third
            else:
                a, b = slopes(third.astype(jnp.int32))
                slope[0, own, pl.ds(PAD + r, 8), :] = a
                slope[1, own, pl.ds(PAD + r, 8), :] = b
        return 0

    chunks = (rows + 2 * HALO) // 8
    lax.fori_loop(0, chunks, unpack, 0)
    for t in range(own):
        for r in (PAD, BASE + rows):
            a, b = slopes(ext[5, t, pl.ds(r, 8), :].astype(jnp.int32))
            slope[0, t, pl.ds(r, 8), :] = a
            slope[1, t, pl.ds(r, 8), :] = b

    def shift_east(x):
        r = [pltpu.roll(a, LANES - 1, 1) for a in x]
        return [jnp.where(lane == LANES - 1, r[(t + 1) % nt], r[t]) for t in range(nt)]

    def shift_west(x):
        r = [pltpu.roll(a, 1, 1) for a in x]
        return [jnp.where(lane == 0, r[t - 1], r[t]) for t in range(nt)]

    def rows_of(ref, f, r):
        return [ref[f, t, pl.ds(r, 8), :] for t in range(nt)]

    def coefs(i, _):
        r = pl.multiple_of(PAD + i * 8, 8)
        m0, u0, v0 = rows_of(ext, 4, r), rows_of(ext, 2, r), rows_of(ext, 3, r)
        x0, y0 = rows_of(slope, 0, r), rows_of(slope, 1, r)
        m1, v1 = rows_of(ext, 4, r + 1), rows_of(ext, 3, r + 1)
        x1, y1 = rows_of(slope, 0, r + 1), rows_of(slope, 1, r + 1)
        me, ue, xe, ye = shift_east(m0), shift_east(u0), shift_east(x0), shift_east(y0)
        for t in range(nt):
            for d, (ma, mb, wa, wb, aa, ab, ba, bb) in enumerate((
                    (m0, me, u0, ue, x0, xe, y0, ye),
                    (m0, m1, v0, v1, y0, y1, x0, x1))):
                m = ma[t] * mb[t]
                vel = 0.5 * (wa[t] + wb[t])
                sa = 0.5 * (aa[t] + ab[t])
                sb = 0.5 * (ba[t] + bb[t])
                speed = jnp.abs(vel)
                coef[4 * d, t, pl.ds(r, 8), :] = m * (0.1 * (1.0 + sa * sa) - jnp.minimum(vel, 0.0))
                coef[4 * d + 1, t, pl.ds(r, 8), :] = m * (0.025 * (sa * sb))
                coef[4 * d + 2, t, pl.ds(r, 8), :] = m * vel
                coef[4 * d + 3, t, pl.ds(r, 8), :] = m * (0.5 * speed * (1.0 - speed))
        return 0

    lax.fori_loop(0, chunks, coefs, 0)

    def limited(dn, du):
        return jnp.maximum(jnp.minimum(dn, du), jnp.minimum(jnp.maximum(dn, du), 0.0))

    def stepped(src, f, r, masked, k):
        qm, q0, q1, q2 = [rows_of(src, f, r + j) for j in (-1, 0, 1, 2)]
        ts = range(nt)
        qe = shift_east(q0)
        dn = [qe[t] - q0[t] for t in ts]
        dw, de = shift_west(dn), shift_east(dn)
        vert = [q1[t] - qm[t] for t in ts]
        ve = shift_east(vert)
        gx = []
        for t in ts:
            lim = limited(dn[t], jnp.where(k[2][t] > 0, dw[t], de[t]))
            gx.append(k[0][t] * dn[t] + k[1][t] * (vert[t] + ve[t]) - (k[2][t] * q0[t] + k[3][t] * lim))
        gw = shift_west(gx)
        pair = [q0[t] + q1[t] for t in ts]
        pe, pw = shift_east(pair), shift_west(pair)
        new = []
        for t in ts:
            dn = q1[t] - q0[t]
            lim = limited(dn, jnp.where(k[6][t] > 0, q0[t] - qm[t], q2[t] - q1[t]))
            g = k[4][t] * dn + k[5][t] * (pe[t] - pw[t]) - (k[6][t] * q0[t] + k[7][t] * lim)
            gy[f, t, pl.ds(r, 8), :] = g
            centre = q0[t] * masked[t] if masked is not None else q0[t]
            new.append(centre + (gx[t] - gw[t]) + g)
        return [new[t] - gy[f, t, pl.ds(r - 1, 8), :] for t in ts]

    def advance(step, src, dst, r):
        k = [rows_of(coef, j, r) for j in range(8)]
        masked = rows_of(ext, 4, r) if step == 0 else None
        for f in range(2):
            new = stepped(src, f, r, masked, k)
            if step < STEPS - 1:
                for t in range(nt):
                    dst[f, t, pl.ds(r, 8), :] = new[t]
            else:
                out = (t_out, s_out)[f]
                for t in range(own):
                    out[pl.ds(pl.multiple_of(r - BASE, 8), 8), pl.ds(LANES * t, LANES)] = new[t]

    pairs = ((ext, qb), (qb, ext))
    for step in range(STEPS):
        src, dst = pairs[step % 2]
        if step < STEPS - 1:
            def body(i, _, step=step, src=src, dst=dst):
                advance(step, src, dst, pl.multiple_of(PAD + i * 8, 8))
                return 0
            lax.fori_loop(0, chunks, body, 0)
        else:
            k = [rows_of(coef, j, PAD) for j in range(8)]
            for f in range(2):
                stepped(src, f, PAD, None, k)

            def body(i, _, step=step, src=src, dst=dst):
                advance(step, src, dst, pl.multiple_of(BASE + i * 8, 8))
                return 0
            lax.fori_loop(0, rows // 8, body, 0)

    to_east.wait_send()
    to_west.wait_send()

    @pl.when(top)
    def _():
        mirror.wait_send()

        @pl.when(fold_e != lon)
        def _():
            mirror_e.wait_send()

        @pl.when(fold_w != lon)
        def _():
            mirror_w.wait_send()

    @pl.when(jnp.logical_not(top))
    def _():
        for c in north:
            c.wait_send()

    @pl.when(jnp.logical_not(low))
    def _():
        for c in south:
            c.wait_send()


def local(nlat, nlon, *args):
    rows, cols = args[0].shape
    nt = cols // LANES + 1
    tall = rows + 2 * BASE
    f32 = jnp.float32
    any_ = pl.BlockSpec(memory_space=pl.ANY)
    vmem = pl.BlockSpec(memory_space=pltpu.VMEM)
    return pl.pallas_call(
        functools.partial(kernel, nlat, nlon),
        out_shape=(jax.ShapeDtypeStruct((rows, cols), f32),) * 2,
        in_specs=[any_, any_, any_, any_, pl.BlockSpec(memory_space=pltpu.SMEM), any_, any_],
        out_specs=(vmem, vmem),
        scratch_shapes=[
            pltpu.VMEM((FIELDS, nt, tall, LANES), f32),
            pltpu.VMEM((2, nt, tall, LANES), f32),
            pltpu.VMEM((2, nt - 1, rows, LANES), jnp.int32),
            pltpu.VMEM((2, nt, tall, LANES), f32),
            pltpu.VMEM((8, nt, tall, LANES), f32),
            pltpu.VMEM((2, nt, tall, LANES), f32),
            pltpu.VMEM((rows, LANES), f32),
            pltpu.VMEM((LANES, rows), f32),
            pltpu.VMEM((PACKED, cols), f32),
            pltpu.VMEM((PACKED, cols), f32),
            pltpu.VMEM((LANES, rows), f32),
            pltpu.VMEM((PACKED, cols), f32),
            pltpu.VMEM((PACKED, cols), f32),
            pltpu.VMEM((4, 8, LANES), f32),
            pltpu.VMEM((rows + 2 * HALO, LANES), f32),
            pltpu.SemaphoreType.DMA((FIELDS * (nt - 1),)),
            pltpu.SemaphoreType.DMA((8,)),
            pltpu.SemaphoreType.DMA((8,)),
        ],
        compiler_params=pltpu.CompilerParams(
            collective_id=0, has_side_effects=True, vmem_limit_bytes=48 * 1024 * 1024),
        name="tracer_steps",
    )(*args)


def solution(mesh):
    names = dict(zip(mesh.axis_names, mesh.devices.shape))
    block = P("lat", "lon")
    return jax.shard_map(
        functools.partial(local, names["lat"], names["lon"]),
        mesh=mesh,
        in_specs=(block, block, block, block, P(), block, block),
        out_specs=(block, block),
        check_vma=False,
    )
```

time: 251 us -> 58.8 us (0.23)
  blocking collectives: 96.9 us -> 0 us
  starting transfers between devices: 53.4 us -> 0 us
  Pallas kernels: 0 us -> 50 us
  waiting for transfers between devices: 46.7 us -> 0 us
  other arithmetic: 39.4 us -> 0 us
  local copies, waits for them, and re-layouts: 12.2 us -> 7.86 us
    all_gather x4 -> x0, blocking collectives: 96.9 us -> none  [mirror_rows(): every = lax.all_gather(top_rows[None], 'lon', axis=0, tiled=True)]
    ppermute x16 -> x0, starting transfers between devices: 53.4 us -> none  [the longest x8 38.6 us: padded(): lax.ppermute(lax.slice_in_dim(block, block.shape[dim] - width, None, axis...]
    pallas_call x0 -> x1, Pallas kernels: none -> 50 us  [local(): pl.pallas_call(functools.partial(kernel, nlat, nlon), out_shape=(jax.Shap...]
    ppermute x16 -> x0, waiting for transfers between devices: 46.7 us -> none  [the longest x8 42.1 us: padded(): lax.ppermute(lax.slice_in_dim(block, 0, width, axis=dim), axis, backward)]
    unnamed x3 -> x0, other arithmetic: 23.5 us -> none
    mul x14 -> x0, other arithmetic: 10.3 us -> none  [the longest x10 9.37 us: face_flux_terms(): lower_mask * upper_mask]
    slice x13 -> x0, local copies, waits for them, and re-layouts: 7.75 us -> none  [the longest x2 3.95 us: local(): gradient_kind_table[klass, 1]]
    unnamed x105 -> x15, local copies, waits for them, and re-layouts: 1.01 us -> 7.86 us
  transfers between devices with their start and end apart: 16 -> 0, of which waited for: 8 -> 0; matrix products, arithmetic and copies ran while one was open for 1% -> 0% of each run, Pallas kernels for 0% -> 0%
where the time goes in v1:
time: 58.8 us; the launch traced here: 58.5 us
  Pallas kernels  50 us (85%)
  local copies, waits for them, and re-layouts  7.86 us (13%)
  between operations  0.64 us (1%)
    pallas_call x1, Pallas kernels, local(): pl.pallas_call(functools.partial(kernel, nlat, nlon), out_shape=(jax.Shap...  50 us
    unnamed x15, local copies, waits for them, and re-layouts  7.86 us

profile of v1, /device:TPU:1, one launch (start us, length us, event | category | flops | bytes accessed | tf_op | source)
XLA Modules:
  0.0 58.5 jit_solution(17574976374660096473)
XLA Ops:
  0.6 0.8 %copy.9.table = f32[16,2]{1,0:T(8,128)S(1)} copy(f32[16,2]{0,1:T(2,128)} %param.11) | data formatting | bytes 256 | tf_op args[4]
  1.4 0.0 copy-start
  1.4 0.9 %copy-done = f32[256,256]{1,0:T(8,128)S(1)} copy-done((f32[256,256]{1,0:T(8,128)S(1)}, f32[256,256]{1,0:T(8,128)}, u32[]{:S(2)}) %copy-start) | copy-done | bytes 262168
  2.3 0.0 copy-start.1
  2.3 0.9 %copy-done.1 = f32[256,256]{1,0:T(8,128)S(1)} copy-done((f32[256,256]{1,0:T(8,128)S(1)}, f32[256,256]{1,0:T(8,128)}, u32[]{:S(2)}) %copy-start.1) | copy-done | bytes 262168
  3.3 0.0 copy-start.2
  3.3 0.9 %copy-done.2 = s32[256,256]{1,0:T(8,128)S(1)} copy-done((s32[256,256]{1,0:T(8,128)S(1)}, s32[256,256]{1,0:T(8,128)}, u32[]{:S(2)}) %copy-start.2) | copy-done | bytes 262168
  4.2 0.0 copy-start.3
  4.2 0.9 %copy-done.3 = s32[256,256]{1,0:T(8,128)S(1)} copy-done((s32[256,256]{1,0:T(8,128)S(1)}, s32[256,256]{1,0:T(8,128)}, u32[]{:S(2)}) %copy-start.3) | copy-done | bytes 262168
  5.2 0.0 copy-start.4
  5.2 0.9 %copy-done.4 = f32[256,256]{1,0:T(8,128)S(1)} copy-done((f32[256,256]{1,0:T(8,128)S(1)}, f32[256,256]{1,0:T(8,128)}, u32[]{:S(2)}) %copy-start.4) | copy-done | bytes 262168
  6.1 0.0 copy-start.5
  6.1 0.9 %copy-done.5 = f32[256,256]{1,0:T(8,128)S(1)} copy-done((f32[256,256]{1,0:T(8,128)S(1)}, f32[256,256]{1,0:T(8,128)}, u32[]{:S(2)}) %copy-start.5) | copy-done | bytes 262168
  7.1 50.0 %tracer_steps.1 = (f32[256,256]{1,0:T(8,128)S(1)}, f32[256,256]{1,0:T(8,128)S(1)}) custom-call(f32[256,256]{1,0:T(8,128)S(1)} %copy-done, f32[256,256]{1,0:T(8,128)S(1)} %copy-done.1, s32[256,256]{1,0:T(8,128)S(1)} %copy-done.2, s32[256,256]{1,0:T(8,128)S(1)} %copy-done.3, f32[16,2]{1,0:T(8,128)S(1)} %copy.9.table, f32[256,256]{1,0:T(8,128)S(1)} %copy-done.4, ...), custom_call_target="tpu_custom_call" | custom-call | tf_op jit(solution)/shard_map/tracer_steps/pallas_call | solution.py:435
  57.1 0.7 %copy.12 = f32[256,256]{1,0:T(8,128)} copy(f32[256,256]{1,0:T(8,128)S(1)} %get-tuple-element.4) | data formatting | bytes 524288
  57.8 0.7 %copy.13 = f32[256,256]{1,0:T(8,128)} copy(f32[256,256]{1,0:T(8,128)S(1)} %get-tuple-element.5) | data formatting | bytes 524288
Async XLA Ops:
  1.4 0.9 %copy-start = (f32[256,256]{1,0:T(8,128)S(1)}, f32[256,256]{1,0:T(8,128)}, u32[]{:S(2)}) copy-start(f32[256,256]{1,0:T(8,128)} %t_in.1) | copy-start | bytes 786436
  2.3 0.9 %copy-start.1 = (f32[256,256]{1,0:T(8,128)S(1)}, f32[256,256]{1,0:T(8,128)}, u32[]{:S(2)}) copy-start(f32[256,256]{1,0:T(8,128)} %s_in.1) | copy-start | bytes 786436
  3.3 0.9 %copy-start.2 = (s32[256,256]{1,0:T(8,128)S(1)}, s32[256,256]{1,0:T(8,128)}, u32[]{:S(2)}) copy-start(s32[256,256]{1,0:T(8,128)} %m_in.1) | copy-start | bytes 786436
  4.2 0.9 %copy-start.3 = (s32[256,256]{1,0:T(8,128)S(1)}, s32[256,256]{1,0:T(8,128)}, u32[]{:S(2)}) copy-start(s32[256,256]{1,0:T(8,128)} %k_in.1) | copy-start | bytes 786436
  5.2 0.9 %copy-start.4 = (f32[256,256]{1,0:T(8,128)S(1)}, f32[256,256]{1,0:T(8,128)}, u32[]{:S(2)}) copy-start(f32[256,256]{1,0:T(8,128)} %u_in.1) | copy-start | bytes 786436
  6.1 0.9 %copy-start.5 = (f32[256,256]{1,0:T(8,128)S(1)}, f32[256,256]{1,0:T(8,128)}, u32[]{:S(2)}) copy-start(f32[256,256]{1,0:T(8,128)} %v_in.1) | copy-start | bytes 786436

commit v2 on v1

--- a/solution.py
+++ b/solution.py
@@ -16,6 +16,31 @@
 PACKED = FIELDS * HALO
 HALF = 64
 MESH = pl.DeviceIdType.MESH
+
+
+GROUP = 4
+
+
+def over_chunks(count, group, body):
+    def some(i, _):
+        body([i * group + j for j in range(group)])
+        return 0
+
+    lax.fori_loop(0, count // group, some, 0)
+    if count % group:
+        body(list(range(count - count % group, count)))
+
+
+def each(body):
+    def run(group):
+        for i in group:
+            body(i)
+
+    return run
+
+
+def row_of(r):
+    return r if isinstance(r, int) else pl.multiple_of(r, 8)
 
 
 def lane_index(rows=8):
@@ -97,8 +122,8 @@
 
     lane = lane_index()
 
-    def pack_rows(i, _):
-        r = pl.multiple_of(i * 8, 8)
+    def pack_rows(i):
+        r = row_of(i * 8)
         out = jnp.zeros((8, LANES), jnp.float32)
         for f in range(FIELDS):
             if f < 4:
@@ -116,9 +141,8 @@
             out = jnp.where((lane >= b) & (lane < b + HALO),
                             pltpu.roll(last, (b - (LANES - HALO)) % LANES, 1), out)
         pack[pl.ds(r, 8), :] = out
-        return 0
-
-    lax.fori_loop(0, rows // 8, pack_rows, 0)
+
+    over_chunks(rows // 8, GROUP, each(pack_rows))
     for h in range(rows // LANES):
         pack_t[:, pl.ds(LANES * h, LANES)] = pack[pl.ds(LANES * h, LANES), :].T
     for f in range(FIELDS):
@@ -190,12 +214,12 @@
         for c in south:
             c.start()
 
-    nclass = table.shape[0]
+    nclass = table.shape[1]
 
     def slopes(idx):
         res = []
         for d in range(2):
-            vals = [table[k, d] for k in range(nclass)]
+            vals = [table[d, k] for k in range(nclass)]
             bit = 1
             while len(vals) > 1:
                 on = (idx & bit) != 0
@@ -205,15 +229,14 @@
             res.append(vals[0])
         return res
 
-    def own_slopes(i, _):
-        r = pl.multiple_of(i * 8, 8)
+    def own_slopes(i):
+        r = row_of(i * 8)
         for t in range(own):
             a, b = slopes(ints[1, t, pl.ds(r, 8), :])
             slope[0, t, pl.ds(BASE + r, 8), :] = a
             slope[1, t, pl.ds(BASE + r, 8), :] = b
-        return 0
-
-    lax.fori_loop(0, rows // 8, own_slopes, 0)
+
+    over_chunks(rows // 8, GROUP, each(own_slopes))
 
     to_east.wait_recv()
     to_west.wait_recv()
@@ -282,8 +305,8 @@
         flipped = ((lane & 63) >= 2 * HALO) & ((lane & 63) < 4 * HALO)
         comb[pl.ds(HALO + rows, 8), :] = jnp.where(flipped, -mixed, mixed)
 
-    def unpack(i, _):
-        r = pl.multiple_of(i * 8, 8)
+    def unpack(i):
+        r = row_of(i * 8)
         both = comb[pl.ds(r, 8), :]
         for f in range(FIELDS):
             a = pltpu.roll(both, (-HALO * f) % LANES, 1) if f else both
@@ -295,10 +318,9 @@
                 a, b = slopes(third.astype(jnp.int32))
                 slope[0, own, pl.ds(PAD + r, 8), :] = a
                 slope[1, own, pl.ds(PAD + r, 8), :] = b
-        return 0
 
     chunks = (rows + 2 * HALO) // 8
-    lax.fori_loop(0, chunks, unpack, 0)
+    over_chunks(chunks, GROUP, each(unpack))
     for t in range(own):
         for r in (PAD, BASE + rows):
             a, b = slopes(ext[5, t, pl.ds(r, 8), :].astype(jnp.int32))
@@ -316,8 +338,8 @@
     def rows_of(ref, f, r):
         return [ref[f, t, pl.ds(r, 8), :] for t in range(nt)]
 
-    def coefs(i, _):
-        r = pl.multiple_of(PAD + i * 8, 8)
+    def coefs(i):
+        r = row_of(PAD + i * 8)
         m0, u0, v0 = rows_of(ext, 4, r), rows_of(ext, 2, r), rows_of(ext, 3, r)
         x0, y0 = rows_of(slope, 0, r), rows_of(slope, 1, r)
         m1, v1 = rows_of(ext, 4, r + 1), rows_of(ext, 3, r + 1)
@@ -336,68 +358,76 @@
                 coef[4 * d + 1, t, pl.ds(r, 8), :] = m * (0.025 * (sa * sb))
                 coef[4 * d + 2, t, pl.ds(r, 8), :] = m * vel
                 coef[4 * d + 3, t, pl.ds(r, 8), :] = m * (0.5 * speed * (1.0 - speed))
-        return 0
-
-    lax.fori_loop(0, chunks, coefs, 0)
+
+    over_chunks(chunks, GROUP, each(coefs))
 
     def limited(dn, du):
         return jnp.maximum(jnp.minimum(dn, du), jnp.minimum(jnp.maximum(dn, du), 0.0))
 
-    def stepped(src, f, r, masked, k):
+    def shift_two(x):
+        r = [pltpu.roll(a, LANES - 2, 1) for a in x]
+        return [jnp.where(lane >= LANES - 2, r[(t + 1) % nt], r[t]) for t in range(nt)]
+
+    def lat_flux(f, r, k, qm, q0, q1, q2, pe, pw, t):
+        dn = q1[t] - q0[t]
+        lim = limited(dn, jnp.where(k[2][t] > 0, q0[t] - qm[t], q2[t] - q1[t]))
+        g = k[0][t] * dn + k[1][t] * (pe[t] - pw[t]) - (k[2][t] * q0[t] + k[3][t] * lim)
+        gy[f, t, pl.ds(r, 8), :] = g
+        return g
+
+    def stepped(src, f, r, masked, k, keep):
         qm, q0, q1, q2 = [rows_of(src, f, r + j) for j in (-1, 0, 1, 2)]
         ts = range(nt)
-        qe = shift_east(q0)
-        dn = [qe[t] - q0[t] for t in ts]
-        dw, de = shift_west(dn), shift_east(dn)
+        qe, qw, qf = shift_east(q0), shift_west(q0), shift_two(q0)
         vert = [q1[t] - qm[t] for t in ts]
         ve = shift_east(vert)
+        pair = [q0[t] + q1[t] for t in ts]
+        pe, pw = shift_east(pair), shift_west(pair)
         gx = []
         for t in ts:
-            lim = limited(dn[t], jnp.where(k[2][t] > 0, dw[t], de[t]))
-            gx.append(k[0][t] * dn[t] + k[1][t] * (vert[t] + ve[t]) - (k[2][t] * q0[t] + k[3][t] * lim))
+            dn = qe[t] - q0[t]
+            lim = limited(dn, jnp.where(k[2][t] > 0, q0[t] - qw[t], qf[t] - qe[t]))
+            gx.append(k[0][t] * dn + k[1][t] * (vert[t] + ve[t]) - (k[2][t] * q0[t] + k[3][t] * lim))
         gw = shift_west(gx)
-        pair = [q0[t] + q1[t] for t in ts]
-        pe, pw = shift_east(pair), shift_west(pair)
         new = []
-        for t in ts:
-            dn = q1[t] - q0[t]
-            lim = limited(dn, jnp.where(k[6][t] > 0, q0[t] - qm[t], q2[t] - q1[t]))
-            g = k[4][t] * dn + k[5][t] * (pe[t] - pw[t]) - (k[6][t] * q0[t] + k[7][t] * lim)
-            gy[f, t, pl.ds(r, 8), :] = g
+        for t in range(keep):
+            g = lat_flux(f, r, k[4:], qm, q0, q1, q2, pe, pw, t)
             centre = q0[t] * masked[t] if masked is not None else q0[t]
             new.append(centre + (gx[t] - gw[t]) + g)
-        return [new[t] - gy[f, t, pl.ds(r - 1, 8), :] for t in ts]
-
-    def advance(step, src, dst, r):
-        k = [rows_of(coef, j, r) for j in range(8)]
-        masked = rows_of(ext, 4, r) if step == 0 else None
-        for f in range(2):
-            new = stepped(src, f, r, masked, k)
-            if step < STEPS - 1:
-                for t in range(nt):
-                    dst[f, t, pl.ds(r, 8), :] = new[t]
-            else:
-                out = (t_out, s_out)[f]
-                for t in range(own):
-                    out[pl.ds(pl.multiple_of(r - BASE, 8), 8), pl.ds(LANES * t, LANES)] = new[t]
+        return new
+
+    def advance(step, src, dst, first, group):
+        last = step == STEPS - 1
+        keep = own if last else nt
+        found = []
+        for i in group:
+            r = row_of(first + i * 8)
+            k = [rows_of(coef, j, r) for j in range(8)]
+            masked = rows_of(ext, 4, r) if step == 0 else None
+            for f in range(2):
+                found.append((f, r, stepped(src, f, r, masked, k, keep)))
+        for f, r, new in found:
+            for t in range(keep):
+                value = new[t] - gy[f, t, pl.ds(r - 1, 8), :]
+                if last:
+                    (t_out, s_out)[f][pl.ds(row_of(r - BASE), 8), pl.ds(LANES * t, LANES)] = value
+                else:
+                    dst[f, t, pl.ds(r, 8), :] = value
 
     pairs = ((ext, qb), (qb, ext))
     for step in range(STEPS):
         src, dst = pairs[step % 2]
         if step < STEPS - 1:
-            def body(i, _, step=step, src=src, dst=dst):
-                advance(step, src, dst, pl.multiple_of(PAD + i * 8, 8))
-                return 0
-            lax.fori_loop(0, chunks, body, 0)
+            over_chunks(chunks, GROUP, functools.partial(advance, step, src, dst, PAD))
         else:
-            k = [rows_of(coef, j, PAD) for j in range(8)]
+            k = [rows_of(coef, j, PAD) for j in range(4, 8)]
             for f in range(2):
-                stepped(src, f, PAD, None, k)
-
-            def body(i, _, step=step, src=src, dst=dst):
-                advance(step, src, dst, pl.multiple_of(BASE + i * 8, 8))
-                return 0
-            lax.fori_loop(0, rows // 8, body, 0)
+                qm, q0, q1, q2 = [rows_of(src, f, PAD + j) for j in (-1, 0, 1, 2)]
+                pair = [q0[t] + q1[t] for t in range(nt)]
+                pe, pw = shift_east(pair), shift_west(pair)
+                for t in range(own):
+                    lat_flux(f, PAD, k, qm, q0, q1, q2, pe, pw, t)
+            over_chunks(rows // 8, GROUP, functools.partial(advance, step, src, dst, BASE))
 
     to_east.wait_send()
     to_west.wait_send()
@@ -430,7 +460,7 @@
     nt = cols // LANES + 1
     tall = rows + 2 * BASE
     f32 = jnp.float32
-    any_ = pl.BlockSpec(memory_space=pl.ANY)
+    any_ = pl.BlockSpec(memory_space=pltpu.HBM)
     vmem = pl.BlockSpec(memory_space=pltpu.VMEM)
     return pl.pallas_call(
         functools.partial(kernel, nlat, nlon),
@@ -458,9 +488,9 @@
             pltpu.SemaphoreType.DMA((8,)),
         ],
         compiler_params=pltpu.CompilerParams(
-            collective_id=0, has_side_effects=True, vmem_limit_bytes=48 * 1024 * 1024),
+            collective_id=0, has_side_effects=True, vmem_limit_bytes=64 * 1024 * 1024 - 65536),
         name="tracer_steps",
-    )(*args)
+    )(*args[:4], args[4].T, *args[5:])
 
 
 def solution(mesh):

time: 58.8 us -> 30 us (0.51)
  Pallas kernels: 50 us -> 26.7 us
  local copies, waits for them, and re-layouts: 7.86 us -> 2.42 us
    pallas_call x1, Pallas kernels: 50 us -> 26.7 us  [local(): pl.pallas_call(functools.partial(kernel, nlat, nlon), out_shape=(jax.Shap...]
    unnamed x15 -> x4, local copies, waits for them, and re-layouts: 7.86 us -> 2.42 us
where the time goes in v2:
time: 30 us; the launch traced here: 29.8 us
  Pallas kernels  26.7 us (89%)
  local copies, waits for them, and re-layouts  2.42 us (8%)
  between operations  0.65 us (2%)
    pallas_call x1, Pallas kernels, local(): pl.pallas_call(functools.partial(kernel, nlat, nlon), out_shape=(jax.Shap...  26.7 us
    unnamed x4, local copies, waits for them, and re-layouts  2.42 us

profile of v2, /device:TPU:1, one launch (start us, length us, event | category | flops | bytes accessed | tf_op | source)
XLA Modules:
  0.0 29.8 jit_solution(13946715493338116894)
XLA Ops:
  0.6 26.7 %tracer_steps.1 = (f32[256,256]{1,0:T(8,128)}, f32[256,256]{1,0:T(8,128)}) custom-call(f32[256,256]{1,0:T(8,128)} %t_in.1, f32[256,256]{1,0:T(8,128)} %s_in.1, s32[256,256]{1,0:T(8,128)} %m_in.1, s32[256,256]{1,0:T(8,128)} %k_in.1, f32[2,16]{1,0:T(2,128)} %bitcast.1, f32[256,256]{1,0:T(8,128)} %u_in.1, f32[256,256]{1,0:T(8,128)} %v_in.1), custom_call_target="tpu_custom_call" | custom-call | tf_op jit(solution)/shard_map/tracer_steps/pallas_call | solution.py:465
  27.3 0.0 copy-start
  27.4 1.7 %copy.11 = f32[256,256]{1,0:T(8,128)} copy(f32[256,256]{1,0:T(8,128)} %get-tuple-element.4) | data formatting | bytes 524288
  29.1 0.0 copy-done
  29.1 0.7 %copy.12 = f32[256,256]{1,0:T(8,128)} copy(f32[256,256]{1,0:T(8,128)S(1)} %copy-done) | data formatting | bytes 524288
Async XLA Ops:
  27.3 1.7 %copy-start = (f32[256,256]{1,0:T(8,128)S(1)}, f32[256,256]{1,0:T(8,128)}, u32[]{:S(2)}) copy-start(f32[256,256]{1,0:T(8,128)} %get-tuple-element.5) | copy-start | bytes 786436

commit v3 on v2

v3 whole, which is shorter than its diff:
```python
import functools

import jax
import jax.numpy as jnp
from jax import lax
from jax.experimental import pallas as pl
from jax.experimental.pallas import tpu as pltpu
from jax.sharding import PartitionSpec as P

STEPS = 4
HALO = 2 * STEPS
FIELDS = 6
LANES = 128
PAD = 8
BASE = PAD + HALO
PACKED = FIELDS * HALO
HALF = 64
MESH = pl.DeviceIdType.MESH


GROUP = 4
STRIP_GROUP = 17


def over_chunks(first, count, group, body):
    def some(i, _):
        body([first + i * group + j for j in range(group)])
        return 0

    lax.fori_loop(0, count // group, some, 0)
    if count % group:
        body([first + count - count % group + j for j in range(count % group)])


def each(body):
    def run(group):
        for i in group:
            body(i)

    return run


def row_of(r):
    return r if isinstance(r, int) else pl.multiple_of(r, 8)


def lane_index(rows=8):
    return lax.broadcasted_iota(jnp.int32, (rows, LANES), 1)


def kernel(
    nlat, nlon,
    t_in, s_in, m_in, k_in, table, u_in, v_in,
    t_out, s_out,
    q, stat, slope, ints, coef, gy,
    pack, pack_t, tops, bots,
    col_t, nbuf, sbuf, corner, comb,
    load_sem, send_sem, recv_sem,
):
    rows, cols = t_in.shape
    own = cols // LANES
    edge = own
    lat = lax.axis_index("lat")
    lon = lax.axis_index("lon")
    top = lat == nlat - 1
    low = lat == 0
    east = lax.rem(lon + 1, nlon)
    west = lax.rem(lon + nlon - 1, nlon)
    fold = nlon - 1 - lon
    fold_e = lax.rem(2 * nlon - 2 - lon, nlon)
    fold_w = lax.rem(nlon - lon, nlon)

    def field_at(f):
        return q.at[0, f] if f < 2 else stat.at[f - 2]

    loads = []
    for f, ref in enumerate((t_in, s_in, u_in, v_in)):
        for t in range(own):
            loads.append(pltpu.make_async_copy(
                ref.at[:, pl.ds(LANES * t, LANES)],
                field_at(f).at[t, pl.ds(BASE, rows), :],
                load_sem.at[len(loads)]))
    for f, ref in enumerate((m_in, k_in)):
        for t in range(own):
            loads.append(pltpu.make_async_copy(
                ref.at[:, pl.ds(LANES * t, LANES)],
                ints.at[f, t],
                load_sem.at[len(loads)]))
    for c in loads:
        c.start()

    barrier = pltpu.get_barrier_semaphore()

    def greet(a, o):
        pl.semaphore_signal(barrier, inc=1, device_id=(o, a), device_id_type=MESH)

    greet(lat, east)
    greet(lat, west)

    @pl.when(jnp.logical_not(top))
    def _():
        greet(lat + 1, lon)
        greet(lat + 1, east)
        greet(lat + 1, west)

    @pl.when(jnp.logical_not(low))
    def _():
        greet(lat - 1, lon)
        greet(lat - 1, east)
        greet(lat - 1, west)

    @pl.when(top)
    def _():
        greet(lat, fold)

        @pl.when(fold_e != lon)
        def _():
            greet(lat, fold_e)

        @pl.when(fold_w != lon)
        def _():
            greet(lat, fold_w)

    for c in loads:
        c.wait()

    lane = lane_index()

    def pack_rows(i):
        r = row_of(i * 8)
        out = jnp.zeros((8, LANES), jnp.float32)
        for f in range(FIELDS):
            if f < 4:
                first = field_at(f)[0, pl.ds(BASE + r, 8), :]
                last = field_at(f)[own - 1, pl.ds(BASE + r, 8), :]
            else:
                parts = [ints[f - 4, t, pl.ds(r, 8), :].astype(jnp.float32) for t in range(own)]
                for t in range(own):
                    field_at(f)[t, pl.ds(BASE + r, 8), :] = parts[t]
                first, last = parts[0], parts[-1]
            a = HALO * f
            b = HALF + HALO * f
            out = jnp.where((lane >= a) & (lane < a + HALO),
                            pltpu.roll(first, a, 1) if a else first, out)
            out = jnp.where((lane >= b) & (lane < b + HALO),
                            pltpu.roll(last, (b - (LANES - HALO)) % LANES, 1), out)
        pack[pl.ds(r, 8), :] = out

    over_chunks(0, rows // 8, GROUP, each(pack_rows))
    for h in range(rows // LANES):
        pack_t[:, pl.ds(LANES * h, LANES)] = pack[pl.ds(LANES * h, LANES), :].T
    for f in range(FIELDS):
        for t in range(own):
            tops[pl.ds(8 * f, 8), pl.ds(LANES * t, LANES)] = field_at(f)[t, pl.ds(BASE + rows - 8, 8), :]
            bots[pl.ds(8 * f, 8), pl.ds(LANES * t, LANES)] = field_at(f)[t, pl.ds(BASE, 8), :]

    others = lambda x: jnp.where(x, 1, 0)
    count = 2 + 3 * others(jnp.logical_not(low)) + others(top) * (
        1 + others(fold_e != lon) + others(fold_w != lon)) + 3 * others(jnp.logical_not(top))
    pl.semaphore_wait(barrier, count)

    pack_top = pack.at[pl.ds(rows - 8, 8), :]
    pack_low = pack.at[pl.ds(0, 8), :]
    from_west = col_t.at[pl.ds(HALF, PACKED), :]
    from_east = col_t.at[pl.ds(0, PACKED), :]

    def rdma(src, dst, s, r, a, o):
        return pltpu.make_async_remote_copy(
            src_ref=src, dst_ref=dst, send_sem=send_sem.at[s], recv_sem=recv_sem.at[r],
            device_id=(o, a), device_id_type=MESH)

    to_east = rdma(pack_t.at[pl.ds(HALF, PACKED), :], from_west, 0, 0, lat, east)
    to_west = rdma(pack_t.at[pl.ds(0, PACKED), :], from_east, 1, 1, lat, west)
    north = [
        rdma(tops, sbuf, 2, 3, lat + 1, lon),
        rdma(pack_top, corner.at[1], 3, 5, lat + 1, east),
        rdma(pack_top, corner.at[0], 4, 4, lat + 1, west),
    ]
    mirror = rdma(tops, nbuf, 2, 2, lat, fold)
    mirror_e = rdma(pack_top, corner.at[2], 3, 6, lat, fold_e)
    mirror_w = rdma(pack_top, corner.at[3], 4, 7, lat, fold_w)
    south = [
        rdma(bots, nbuf, 5, 2, lat - 1, lon),
        rdma(pack_low, corner.at[3], 6, 7, lat - 1, east),
        rdma(pack_low, corner.at[2], 7, 6, lat - 1, west),
    ]

    to_east.start()
    to_west.start()

    @pl.when(top)
    def _():
        mirror.start()

        @pl.when(fold_e != lon)
        def _():
            mirror_e.start()

        @pl.when(fold_w != lon)
        def _():
            mirror_w.start()

        @pl.when(fold_e == lon)
        def _():
            corner[2] = pack[pl.ds(rows - 8, 8), :]

        @pl.when(fold_w == lon)
        def _():
            corner[3] = pack[pl.ds(rows - 8, 8), :]

    @pl.when(jnp.logical_not(top))
    def _():
        for c in north:
            c.start()

    @pl.when(jnp.logical_not(low))
    def _():
        for c in south:
            c.start()

    nclass = table.shape[1]

    def slopes(idx):
        res = []
        for d in range(2):
            vals = [table[d, k] for k in range(nclass)]
            bit = 1
            while len(vals) > 1:
                on = (idx & bit) != 0
                vals = [jnp.where(on, vals[j + 1], vals[j]) if j + 1 < len(vals) else vals[j]
                        for j in range(0, len(vals), 2)]
                bit *= 2
            res.append(vals[0])
        return res

    def put_slopes(t, r, idx):
        a, b = slopes(idx)
        slope[0, t, pl.ds(r, 8), :] = a
        slope[1, t, pl.ds(r, 8), :] = b

    chunks = (rows + 2 * HALO) // 8

    def own_slopes(e):
        r = row_of(PAD + e * 8)
        for t in range(own):
            put_slopes(t, r, ints[1, t, pl.ds(row_of(r - BASE), 8), :])

    part = lane & (HALF - 1)
    lower = lane < HALF

    def own_strips(e):
        r = row_of(PAD + e * 8)

        def context(f, o):
            ref = field_at(f)
            a = pltpu.roll(ref[0, pl.ds(r, 8), :], HALO + o, 1)
            b = pltpu.roll(ref[own - 1, pl.ds(r, 8), :], (5 * HALO + o) % LANES, 1)
            return jnp.where(part < 3 * HALO, a, b)

        q[0, 2, 0, pl.ds(r, 8), :] = jnp.where(lower, context(0, 0), context(1, HALF))
        for f in range(2, FIELDS):
            a = context(f, 0)
            stat[f - 2, edge, pl.ds(r, 8), :] = jnp.where(lower, a, pltpu.roll(a, HALF, 1))

    beyond = (part < HALO) | (part >= 5 * HALO)

    def whole_strips(e):
        r = row_of(PAD + e * 8)
        both = comb[pl.ds(row_of(r - PAD), 8), :]

        def halo(f, o):
            a = pltpu.roll(both, (o + HALF - HALO * f) % LANES, 1)
            b = pltpu.roll(both, (o + 5 * HALO - HALO * f) % LANES, 1)
            return jnp.where(part < HALO, a, b)

        z = jnp.where(lower, halo(0, 0), halo(1, HALF))
        q[0, 2, 0, pl.ds(r, 8), :] = jnp.where(beyond, z, q[0, 2, 0, pl.ds(r, 8), :])
        for f in range(2, FIELDS):
            a = halo(f, 0)
            z = jnp.where(lower, a, pltpu.roll(a, HALF, 1))
            z = jnp.where(beyond, z, stat[f - 2, edge, pl.ds(r, 8), :])
            if f < FIELDS - 1:
                stat[f - 2, edge, pl.ds(r, 8), :] = z
            else:
                put_slopes(edge, r, z.astype(jnp.int32))

    def shifted(x, by):
        r = [pltpu.roll(a, (-by) % LANES, 1) for a in x]
        n = len(x)
        if n == 1:
            return r
        if by > 0:
            return [jnp.where(lane >= LANES - by, r[(t + 1) % n], r[t]) for t in range(n)]
        return [jnp.where(lane < -by, r[t - 1], r[t]) for t in range(n)]

    def coefs(tiles, e):
        r = row_of(PAD + e * 8)

        def rows_at(ref, f, at):
            return [ref[f, t, pl.ds(at, 8), :] for t in tiles]

        u0, v0, m0 = [rows_at(stat, f, r) for f in range(3)]
        v1, m1 = [rows_at(stat, f, r + 1) for f in (1, 2)]
        x0, y0 = [rows_at(slope, f, r) for f in range(2)]
        x1, y1 = [rows_at(slope, f, r + 1) for f in range(2)]
        me, ue, xe, ye = [shifted(x, 1) for x in (m0, u0, x0, y0)]
        for j, t in enumerate(tiles):
            for d, (ma, mb, wa, wb, aa, ab, ba, bb) in enumerate((
                    (m0, me, u0, ue, x0, xe, y0, ye),
                    (m0, m1, v0, v1, y0, y1, x0, x1))):
                m = ma[j] * mb[j]
                vel = 0.5 * (wa[j] + wb[j])
                sa = 0.5 * (aa[j] + ab[j])
                sb = 0.5 * (ba[j] + bb[j])
                speed = jnp.abs(vel)
                coef[4 * d, t, pl.ds(r, 8), :] = m * (0.1 * (1.0 + sa * sa) - jnp.minimum(vel, 0.0))
                coef[4 * d + 1, t, pl.ds(r, 8), :] = m * (0.025 * (sa * sb))
                coef[4 * d + 2, t, pl.ds(r, 8), :] = m * vel
                coef[4 * d + 3, t, pl.ds(r, 8), :] = m * (0.5 * speed * (1.0 - speed))

    def limited(dn, du):
        return jnp.maximum(jnp.minimum(dn, du), jnp.minimum(jnp.maximum(dn, du), 0.0))

    def coef_tiles(f):
        return range(own) if f < 2 else (edge,)

    def q_rows(step, f, r):
        return [[q[step, f, t, pl.ds(r + j, 8), :] for t in range(own if f < 2 else 1)]
                for j in (-1, 0, 1, 2)]

    def lat_flux(step, f, r, k, around):
        qm, q0, q1, q2 = around
        pair = [a + b for a, b in zip(q0, q1)]
        pe, pw = shifted(pair, 1), shifted(pair, -1)
        res = []
        for t in range(len(q0)):
            dn = q1[t] - q0[t]
            lim = limited(dn, jnp.where(k[2][t] > 0, q0[t] - qm[t], q2[t] - q1[t]))
            g = k[0][t] * dn + k[1][t] * (pe[t] - pw[t]) - (k[2][t] * q0[t] + k[3][t] * lim)
            gy[step, f, t, pl.ds(r, 8), :] = g
            res.append(g)
        return res

    def lat_only(step, e):
        r = row_of(PAD + e * 8)
        k = [[coef[j, t, pl.ds(r, 8), :] for t in range(own)] for j in range(4, 8)]
        for f in range(2):
            lat_flux(step, f, r, k, q_rows(step, f, r))

    def stepped(step, f, r, k, masked):
        around = q_rows(step, f, r)
        qm, q0, q1, q2 = around
        qe, qw, qf = shifted(q0, 1), shifted(q0, -1), shifted(q0, 2)
        vert = [a - b for a, b in zip(q1, qm)]
        ve = shifted(vert, 1)
        gx = []
        for t in range(len(q0)):
            dn = qe[t] - q0[t]
            lim = limited(dn, jnp.where(k[2][t] > 0, q0[t] - qw[t], qf[t] - qe[t]))
            gx.append(k[0][t] * dn + k[1][t] * (vert[t] + ve[t]) - (k[2][t] * q0[t] + k[3][t] * lim))
        gw = shifted(gx, -1)
        g = lat_flux(step, f, r, k[4:], around)
        new = []
        for t in range(len(q0)):
            centre = q0[t] * masked[t] if masked is not None else q0[t]
            new.append(centre + (gx[t] - gw[t]) + g[t])
        return new

    def advance(step, fields, group):
        found = []
        for e in group:
            r = row_of(PAD + e * 8)
            tiles = coef_tiles(fields[0])
            k = [[coef[j, t, pl.ds(r, 8), :] for t in tiles] for j in range(8)]
            masked = [stat[2, t, pl.ds(r, 8), :] for t in tiles] if step == 0 else None
            for f in fields:
                found.append((f, r, stepped(step, f, r, k, masked)))
        for f, r, new in found:
            for t in range(len(new)):
                value = new[t] - gy[step, f, t, pl.ds(r - 1, 8), :]
                if step == STEPS - 1 and f < 2:
                    (t_out, s_out)[f][pl.ds(row_of(r - BASE), 8), pl.ds(LANES * t, LANES)] = value
                else:
                    q[step + 1, f, t, pl.ds(r, 8), :] = value

    over_chunks(1, rows // 8, GROUP, each(own_slopes))
    over_chunks(1, rows // 8, GROUP, each(own_strips))
    over_chunks(1, rows // 8 - 1, GROUP, each(functools.partial(coefs, range(own))))
    for step in range(STEPS):
        first = step + 2
        lat_only(step, first - 1)
        over_chunks(first, chunks - 2 * first, GROUP, functools.partial(advance, step, (0, 1)))

    to_east.wait_recv()
    to_west.wait_recv()
    for h in range(rows // LANES):
        comb[pl.ds(HALO + LANES * h, LANES), :] = col_t[:, pl.ds(LANES * h, LANES)].T

    @pl.when(low)
    def _():
        comb[pl.ds(0, 8), :] = jnp.zeros((8, LANES), jnp.float32)
        for f in range(FIELDS):
            for t in range(own):
                field_at(f)[t, pl.ds(PAD, 8), :] = jnp.zeros((8, LANES), jnp.float32)

    @pl.when(jnp.logical_not(low))
    def _():
        north[0].wait_recv()
        north[1].wait_recv()
        north[2].wait_recv()
        comb[pl.ds(0, 8), :] = jnp.where(lane < HALF, corner[0], corner[1])
        for f in range(FIELDS):
            for t in range(own):
                field_at(f)[t, pl.ds(PAD, 8), :] = sbuf[pl.ds(8 * f, 8), pl.ds(LANES * t, LANES)]

    mirror.wait_recv()

    @pl.when(jnp.logical_not(top))
    def _():
        mirror_e.wait_recv()
        mirror_w.wait_recv()
        comb[pl.ds(HALO + rows, 8), :] = jnp.where(lane < HALF, corner[2], corner[3])
        for f in range(FIELDS):
            for t in range(own):
                field_at(f)[t, pl.ds(BASE + rows, 8), :] = nbuf[pl.ds(8 * f, 8), pl.ds(LANES * t, LANES)]

    @pl.when(top)
    def _():
        @pl.when(fold_e != lon)
        def _():
            mirror_e.wait_recv()

        @pl.when(fold_w != lon)
        def _():
            mirror_w.wait_recv()

        def dot(a, b):
            return jnp.dot(a, b, precision=lax.Precision.HIGHEST, preferred_element_type=jnp.float32)

        def iotas(n):
            return (lax.broadcasted_iota(jnp.int32, (n, n), 0), lax.broadcasted_iota(jnp.int32, (n, n), 1))

        i, j = iotas(cols)
        flip = jnp.where(i + j == cols - 1, 1.0, 0.0)
        i, j = iotas(PACKED)
        turn = jnp.where(j == i + 7 - 2 * (i & 7), 1.0, 0.0)
        turned = dot(turn, dot(nbuf[...], flip))
        for f in range(FIELDS):
            sign = -1.0 if f in (2, 3) else 1.0
            for t in range(own):
                field_at(f)[t, pl.ds(BASE + rows, 8), :] = sign * turned[8 * f:8 * f + 8, LANES * t:LANES * t + LANES]
        i, j = iotas(LANES)
        swap = jnp.where(i == ((j + HALF) & 127) + 7 - 2 * (j & 7), 1.0, 0.0)
        i, j = iotas(8)
        turn8 = jnp.where(i + j == 7, 1.0, 0.0)
        mixed = jnp.where(lane >= HALF, corner[2], corner[3])
        mixed = dot(turn8, dot(mixed, swap))
        flipped = ((lane & 63) >= 2 * HALO) & ((lane & 63) < 4 * HALO)
        comb[pl.ds(HALO + rows, 8), :] = jnp.where(flipped, -mixed, mixed)

    for t in range(own):
        for r in (PAD, BASE + rows):
            put_slopes(t, r, stat[3, t, pl.ds(r, 8), :].astype(jnp.int32))
    own_strips(0)
    own_strips(chunks - 1)
    over_chunks(0, chunks, 8, each(whole_strips))

    for e in (0, chunks - 2, chunks - 1):
        coefs(range(own), e)
    over_chunks(0, chunks, 8, each(functools.partial(coefs, (edge,))))

    for step in range(STEPS):
        last = step == STEPS - 1
        if last:
            lat_only(step, 0)
        ends = list(range(last, step + 2)) + list(range(chunks - step - 2, chunks - last))
        advance(step, (0, 1), ends)
        over_chunks(0, chunks, STRIP_GROUP, functools.partial(advance, step, (2,)))

    def merge(e):
        r = row_of(PAD + e * 8)
        both = q[STEPS, 2, 0, pl.ds(r, 8), :]
        for f, out in enumerate((t_out, s_out)):
            o = row_of(r - BASE)
            a = pltpu.roll(both, (LANES - HALO - HALF * f) % LANES, 1)
            b = pltpu.roll(both, (LANES - 5 * HALO - HALF * f) % LANES, 1)
            left = pl.ds(0, LANES)
            right = pl.ds(LANES * (own - 1), LANES)
            out[pl.ds(o, 8), left] = jnp.where(lane < HALO, a, out[pl.ds(o, 8), left])
            out[pl.ds(o, 8), right] = jnp.where(lane >= LANES - HALO, b, out[pl.ds(o, 8), right])

    over_chunks(1, rows // 8, 8, each(merge))

    to_east.wait_send()
    to_west.wait_send()

    @pl.when(top)
    def _():
        mirror.wait_send()

        @pl.when(fold_e != lon)
        def _():
            mirror_e.wait_send()

        @pl.when(fold_w != lon)
        def _():
            mirror_w.wait_send()

    @pl.when(jnp.logical_not(top))
    def _():
        for c in north:
            c.wait_send()

    @pl.when(jnp.logical_not(low))
    def _():
        for c in south:
            c.wait_send()


def local(nlat, nlon, *args):
    rows, cols = args[0].shape
    own = cols // LANES
    tall = rows + 2 * BASE
    f32 = jnp.float32
    any_ = pl.BlockSpec(memory_space=pltpu.HBM)
    vmem = pl.BlockSpec(memory_space=pltpu.VMEM)
    return pl.pallas_call(
        functools.partial(kernel, nlat, nlon),
        out_shape=(jax.ShapeDtypeStruct((rows, cols), f32),) * 2,
        in_specs=[any_, any_, any_, any_, pl.BlockSpec(memory_space=pltpu.SMEM), any_, any_],
        out_specs=(vmem, vmem),
        scratch_shapes=[
            pltpu.VMEM((STEPS + 1, 3, own, tall, LANES), f32),
            pltpu.VMEM((4, own + 1, tall, LANES), f32),
            pltpu.VMEM((2, own + 1, tall, LANES), f32),
            pltpu.VMEM((2, own, rows, LANES), jnp.int32),
            pltpu.VMEM((8, own + 1, tall, LANES), f32),
            pltpu.VMEM((STEPS, 3, own, tall, LANES), f32),
            pltpu.VMEM((rows, LANES), f32),
            pltpu.VMEM((LANES, rows), f32),
            pltpu.VMEM((PACKED, cols), f32),
            pltpu.VMEM((PACKED, cols), f32),
            pltpu.VMEM((LANES, rows), f32),
            pltpu.VMEM((PACKED, cols), f32),
            pltpu.VMEM((PACKED, cols), f32),
            pltpu.VMEM((4, 8, LANES), f32),
            pltpu.VMEM((rows + 2 * HALO, LANES), f32),
            pltpu.SemaphoreType.DMA((FIELDS * own,)),
            pltpu.SemaphoreType.DMA((8,)),
            pltpu.SemaphoreType.DMA((8,)),
        ],
        compiler_params=pltpu.CompilerParams(
            collective_id=0, has_side_effects=True, vmem_limit_bytes=64 * 1024 * 1024 - 65536),
        name="tracer_steps",
    )(*args[:4], args[4].T, *args[5:])


def solution(mesh):
    names = dict(zip(mesh.axis_names, mesh.devices.shape))
    block = P("lat", "lon")
    return jax.shard_map(
        functools.partial(local, names["lat"], names["lon"]),
        mesh=mesh,
        in_specs=(block, block, block, block, P(), block, block),
        out_specs=(block, block),
        check_vma=False,
    )
```

time: 30 us -> 26.9 us (0.90)
  Pallas kernels: 26.7 us -> 23.7 us
    pallas_call x1, Pallas kernels: 26.7 us -> 23.7 us  [local(): pl.pallas_call(functools.partial(kernel, nlat, nlon), out_shape=(jax.Shap...]
where the time goes in v3:
time: 26.9 us; the launch traced here: 26.7 us
  Pallas kernels  23.7 us (88%)
  local copies, waits for them, and re-layouts  2.42 us (9%)
  between operations  0.65 us (2%)
    pallas_call x1, Pallas kernels, local(): pl.pallas_call(functools.partial(kernel, nlat, nlon), out_shape=(jax.Shap...  23.7 us
    unnamed x4, local copies, waits for them, and re-layouts  2.42 us

profile of v3, /device:TPU:1, one launch (start us, length us, event | category | flops | bytes accessed | tf_op | source)
XLA Modules:
  0.0 26.7 jit_solution(11513452565086795152)
XLA Ops:
  0.6 23.7 %tracer_steps.1 = (f32[256,256]{1,0:T(8,128)}, f32[256,256]{1,0:T(8,128)}) custom-call(f32[256,256]{1,0:T(8,128)} %t_in.1, f32[256,256]{1,0:T(8,128)} %s_in.1, s32[256,256]{1,0:T(8,128)} %m_in.1, s32[256,256]{1,0:T(8,128)} %k_in.1, f32[2,16]{1,0:T(2,128)} %bitcast.1, f32[256,256]{1,0:T(8,128)} %u_in.1, f32[256,256]{1,0:T(8,128)} %v_in.1), custom_call_target="tpu_custom_call" | custom-call | tf_op jit(solution)/shard_map/tracer_steps/pallas_call | solution.py:527
  24.3 0.0 copy-start
  24.3 1.7 %copy.11 = f32[256,256]{1,0:T(8,128)} copy(f32[256,256]{1,0:T(8,128)} %get-tuple-element.4) | data formatting | bytes 524288
  26.0 0.0 copy-done
  26.0 0.7 %copy.12 = f32[256,256]{1,0:T(8,128)} copy(f32[256,256]{1,0:T(8,128)S(1)} %copy-done) | data formatting | bytes 524288
Async XLA Ops:
  24.3 1.7 %copy-start = (f32[256,256]{1,0:T(8,128)S(1)}, f32[256,256]{1,0:T(8,128)}, u32[]{:S(2)}) copy-start(f32[256,256]{1,0:T(8,128)} %get-tuple-element.5) | copy-start | bytes 786436

commit v4 on v3

--- a/solution.py
+++ b/solution.py
@@ -15,11 +15,14 @@
 BASE = PAD + HALO
 PACKED = FIELDS * HALO
 HALF = 64
+VMEM_BYTES = 64 * 1024 * 1024
 MESH = pl.DeviceIdType.MESH
 
 
-GROUP = 4
+GROUP = 8
+STEP_GROUP = 10
 STRIP_GROUP = 17
+ENDS = STEPS + 1
 
 
 def over_chunks(first, count, group, body):
@@ -362,34 +365,33 @@
         g = lat_flux(step, f, r, k[4:], around)
         new = []
         for t in range(len(q0)):
-            centre = q0[t] * masked[t] if masked is not None else q0[t]
-            new.append(centre + (gx[t] - gw[t]) + g[t])
+            new.append(q0[t] * masked[t] + (gx[t] - gw[t]) + g[t])
         return new
 
-    def advance(step, fields, group):
+    def advance(step, work):
         found = []
-        for e in group:
+        for fields, e in work:
             r = row_of(PAD + e * 8)
             tiles = coef_tiles(fields[0])
             k = [[coef[j, t, pl.ds(r, 8), :] for t in tiles] for j in range(8)]
-            masked = [stat[2, t, pl.ds(r, 8), :] for t in tiles] if step == 0 else None
+            masked = [stat[2, t, pl.ds(r, 8), :] for t in tiles]
             for f in fields:
                 found.append((f, r, stepped(step, f, r, k, masked)))
         for f, r, new in found:
             for t in range(len(new)):
-                value = new[t] - gy[step, f, t, pl.ds(r - 1, 8), :]
-                if step == STEPS - 1 and f < 2:
-                    (t_out, s_out)[f][pl.ds(row_of(r - BASE), 8), pl.ds(LANES * t, LANES)] = value
-                else:
-                    q[step + 1, f, t, pl.ds(r, 8), :] = value
+                q[step + 1, f, t, pl.ds(r, 8), :] = new[t] - gy[step, f, t, pl.ds(r - 1, 8), :]
 
     over_chunks(1, rows // 8, GROUP, each(own_slopes))
     over_chunks(1, rows // 8, GROUP, each(own_strips))
-    over_chunks(1, rows // 8 - 1, GROUP, each(functools.partial(coefs, range(own))))
-    for step in range(STEPS):
-        first = step + 2
-        lat_only(step, first - 1)
-        over_chunks(first, chunks - 2 * first, GROUP, functools.partial(advance, step, (0, 1)))
+    over_chunks(1, rows // 8, GROUP, each(functools.partial(coefs, range(own))))
+
+    def interior(step, _):
+        lat_only(step, 1)
+        over_chunks(2, chunks - 4, STEP_GROUP,
+                    lambda group: advance(step, [((0, 1), e) for e in group]))
+        return 0
+
+    lax.fori_loop(0, STEPS, interior, 0)
 
     to_east.wait_recv()
     to_west.wait_recv()
@@ -463,33 +465,35 @@
             put_slopes(t, r, stat[3, t, pl.ds(r, 8), :].astype(jnp.int32))
     own_strips(0)
     own_strips(chunks - 1)
-    over_chunks(0, chunks, 8, each(whole_strips))
+    over_chunks(0, chunks, STRIP_GROUP, each(whole_strips))
 
     for e in (0, chunks - 2, chunks - 1):
         coefs(range(own), e)
-    over_chunks(0, chunks, 8, each(functools.partial(coefs, (edge,))))
-
-    for step in range(STEPS):
-        last = step == STEPS - 1
-        if last:
-            lat_only(step, 0)
-        ends = list(range(last, step + 2)) + list(range(chunks - step - 2, chunks - last))
-        advance(step, (0, 1), ends)
-        over_chunks(0, chunks, STRIP_GROUP, functools.partial(advance, step, (2,)))
+    over_chunks(0, chunks, STRIP_GROUP, each(functools.partial(coefs, (edge,))))
+
+    def rest(step, _):
+        ends = list(range(ENDS)) + list(range(chunks - ENDS, chunks))
+        advance(step, [((0, 1), e) for e in ends])
+        over_chunks(0, chunks, STRIP_GROUP,
+                    lambda group: advance(step, [((2,), e) for e in group]))
+        return 0
+
+    lax.fori_loop(0, STEPS, rest, 0)
 
     def merge(e):
         r = row_of(PAD + e * 8)
         both = q[STEPS, 2, 0, pl.ds(r, 8), :]
         for f, out in enumerate((t_out, s_out)):
             o = row_of(r - BASE)
+            tiles = [q[STEPS, f, t, pl.ds(r, 8), :] for t in range(own)]
             a = pltpu.roll(both, (LANES - HALO - HALF * f) % LANES, 1)
             b = pltpu.roll(both, (LANES - 5 * HALO - HALF * f) % LANES, 1)
-            left = pl.ds(0, LANES)
-            right = pl.ds(LANES * (own - 1), LANES)
-            out[pl.ds(o, 8), left] = jnp.where(lane < HALO, a, out[pl.ds(o, 8), left])
-            out[pl.ds(o, 8), right] = jnp.where(lane >= LANES - HALO, b, out[pl.ds(o, 8), right])
-
-    over_chunks(1, rows // 8, 8, each(merge))
+            tiles[0] = jnp.where(lane < HALO, a, tiles[0])
+            tiles[-1] = jnp.where(lane >= LANES - HALO, b, tiles[-1])
+            for t in range(own):
+                out[pl.ds(o, 8), pl.ds(LANES * t, LANES)] = tiles[t]
+
+    over_chunks(1, rows // 8, GROUP, each(merge))
 
     to_east.wait_send()
     to_west.wait_send()
@@ -515,6 +519,15 @@
     def _():
         for c in south:
             c.wait_send()
+
+
+def write_out(t_in, s_in, t_out, s_out, sem):
+    copies = [pltpu.make_async_copy(t_in, t_out, sem.at[0]),
+              pltpu.make_async_copy(s_in, s_out, sem.at[1])]
+    for c in copies:
+        c.start()
+    for c in copies:
+        c.wait()
 
 
 def local(nlat, nlon, *args):
@@ -524,9 +537,9 @@
     f32 = jnp.float32
     any_ = pl.BlockSpec(memory_space=pltpu.HBM)
     vmem = pl.BlockSpec(memory_space=pltpu.VMEM)
-    return pl.pallas_call(
+    found = pl.pallas_call(
         functools.partial(kernel, nlat, nlon),
-        out_shape=(jax.ShapeDtypeStruct((rows, cols), f32),) * 2,
+        out_shape=(pltpu.VMEM((rows, cols), f32),) * 2,
         in_specs=[any_, any_, any_, any_, pl.BlockSpec(memory_space=pltpu.SMEM), any_, any_],
         out_specs=(vmem, vmem),
         scratch_shapes=[
@@ -550,9 +563,17 @@
             pltpu.SemaphoreType.DMA((8,)),
         ],
         compiler_params=pltpu.CompilerParams(
-            collective_id=0, has_side_effects=True, vmem_limit_bytes=64 * 1024 * 1024 - 65536),
+            collective_id=0, has_side_effects=True, vmem_limit_bytes=VMEM_BYTES - 2 * rows * cols * 4 - 65536),
         name="tracer_steps",
     )(*args[:4], args[4].T, *args[5:])
+    return pl.pallas_call(
+        write_out,
+        out_shape=(jax.ShapeDtypeStruct((rows, cols), f32),) * 2,
+        in_specs=[pl.BlockSpec(memory_space=pl.ANY)] * 2,
+        out_specs=(pl.BlockSpec(memory_space=pl.ANY),) * 2,
+        scratch_shapes=[pltpu.SemaphoreType.DMA((2,))],
+        name="write_out",
+    )(*found)
 
 
 def solution(mesh):

time: 26.9 us -> 52.6 us (1.96)
  Pallas kernels: 23.7 us -> 50.4 us
  local copies, waits for them, and re-layouts: 2.42 us -> 1.39 us
    pallas_call x1 -> x2, Pallas kernels: 23.7 us -> 50.4 us  [the longest x1 33.4 us: local(): pl.pallas_call(functools.partial(kernel, nlat, nlon), out_shape=(pltpu.VM...]
    unnamed x4, local copies, waits for them, and re-layouts: 2.42 us -> 1.39 us
where the time goes in v4:
time: 52.6 us; the launch traced here: 52.5 us
  Pallas kernels  50.4 us (96%)
  local copies, waits for them, and re-layouts  1.39 us (3%)
  between operations  0.65 us (1%)
    pallas_call x1, Pallas kernels, local(): pl.pallas_call(functools.partial(kernel, nlat, nlon), out_shape=(pltpu.VM...  33.4 us
    pallas_call x1, Pallas kernels, local(): pl.pallas_call(write_out, out_shape=(jax.ShapeDtypeStruct((rows, cols), f...  17 us
    unnamed x4, local copies, waits for them, and re-layouts  1.39 us

profile of v4, /device:TPU:1, one launch (start us, length us, event | category | flops | bytes accessed | tf_op | source)
XLA Modules:
  0.0 52.5 jit_solution(9366140810187992849)
XLA Ops:
  0.6 33.4 %tracer_steps.1 = (f32[256,256]{1,0:T(8,128)S(1)}, f32[256,256]{1,0:T(8,128)S(1)}) custom-call(f32[256,256]{1,0:T(8,128)} %t_in.1, f32[256,256]{1,0:T(8,128)} %s_in.1, s32[256,256]{1,0:T(8,128)} %m_in.1, s32[256,256]{1,0:T(8,128)} %k_in.1, f32[2,16]{1,0:T(2,128)} %bitcast.1, f32[256,256]{1,0:T(8,128)} %u_in.1, f32[256,256]{1,0:T(8,128)} %v_in.1), custom_call_target="tpu_custom_call" | custom-call | tf_op jit(solution)/shard_map/tracer_steps/pallas_call | solution.py:540
  34.1 0.0 copy-start
  34.1 0.7 %copy-done = f32[256,256]{1,0:T(8,128)} copy-done((f32[256,256]{1,0:T(8,128)}, f32[256,256]{1,0:T(8,128)S(1)}, u32[]{:S(2)}) %copy-start) | copy-done | bytes 262168
  34.8 0.0 copy-start.1
  34.8 0.7 %copy-done.1 = f32[256,256]{1,0:T(8,128)} copy-done((f32[256,256]{1,0:T(8,128)}, f32[256,256]{1,0:T(8,128)S(1)}, u32[]{:S(2)}) %copy-start.1) | copy-done | bytes 262168
  35.5 17.0 %write_out.1 = (f32[256,256]{1,0:T(8,128)}, f32[256,256]{1,0:T(8,128)}) custom-call(f32[256,256]{1,0:T(8,128)} %copy-done, f32[256,256]{1,0:T(8,128)} %copy-done.1), custom_call_target="tpu_custom_call" | custom-call | tf_op jit(solution)/shard_map/write_out/pallas_call | solution.py:569
Async XLA Ops:
  34.1 0.7 %copy-start = (f32[256,256]{1,0:T(8,128)}, f32[256,256]{1,0:T(8,128)S(1)}, u32[]{:S(2)}) copy-start(f32[256,256]{1,0:T(8,128)S(1)} %get-tuple-element.4.t_in) | copy-start | bytes 786436
  34.8 0.7 %copy-start.1 = (f32[256,256]{1,0:T(8,128)}, f32[256,256]{1,0:T(8,128)S(1)}, u32[]{:S(2)}) copy-start(f32[256,256]{1,0:T(8,128)S(1)} %get-tuple-element.5.s_in) | copy-start | bytes 786436

commit v5 on v3

--- a/solution.py
+++ b/solution.py
@@ -15,6 +15,7 @@
 BASE = PAD + HALO
 PACKED = FIELDS * HALO
 HALF = 64
+VMEM_BYTES = 64 * 1024 * 1024
 MESH = pl.DeviceIdType.MESH
 
 
@@ -154,70 +155,6 @@
             tops[pl.ds(8 * f, 8), pl.ds(LANES * t, LANES)] = field_at(f)[t, pl.ds(BASE + rows - 8, 8), :]
             bots[pl.ds(8 * f, 8), pl.ds(LANES * t, LANES)] = field_at(f)[t, pl.ds(BASE, 8), :]
 
-    others = lambda x: jnp.where(x, 1, 0)
-    count = 2 + 3 * others(jnp.logical_not(low)) + others(top) * (
-        1 + others(fold_e != lon) + others(fold_w != lon)) + 3 * others(jnp.logical_not(top))
-    pl.semaphore_wait(barrier, count)
-
-    pack_top = pack.at[pl.ds(rows - 8, 8), :]
-    pack_low = pack.at[pl.ds(0, 8), :]
-    from_west = col_t.at[pl.ds(HALF, PACKED), :]
-    from_east = col_t.at[pl.ds(0, PACKED), :]
-
-    def rdma(src, dst, s, r, a, o):
-        return pltpu.make_async_remote_copy(
-            src_ref=src, dst_ref=dst, send_sem=send_sem.at[s], recv_sem=recv_sem.at[r],
-            device_id=(o, a), device_id_type=MESH)
-
-    to_east = rdma(pack_t.at[pl.ds(HALF, PACKED), :], from_west, 0, 0, lat, east)
-    to_west = rdma(pack_t.at[pl.ds(0, PACKED), :], from_east, 1, 1, lat, west)
-    north = [
-        rdma(tops, sbuf, 2, 3, lat + 1, lon),
-        rdma(pack_top, corner.at[1], 3, 5, lat + 1, east),
-        rdma(pack_top, corner.at[0], 4, 4, lat + 1, west),
-    ]
-    mirror = rdma(tops, nbuf, 2, 2, lat, fold)
-    mirror_e = rdma(pack_top, corner.at[2], 3, 6, lat, fold_e)
-    mirror_w = rdma(pack_top, corner.at[3], 4, 7, lat, fold_w)
-    south = [
-        rdma(bots, nbuf, 5, 2, lat - 1, lon),
-        rdma(pack_low, corner.at[3], 6, 7, lat - 1, east),
-        rdma(pack_low, corner.at[2], 7, 6, lat - 1, west),
-    ]
-
-    to_east.start()
-    to_west.start()
-
-    @pl.when(top)
-    def _():
-        mirror.start()
-
-        @pl.when(fold_e != lon)
-        def _():
-            mirror_e.start()
-
-        @pl.when(fold_w != lon)
-        def _():
-            mirror_w.start()
-
-        @pl.when(fold_e == lon)
-        def _():
-            corner[2] = pack[pl.ds(rows - 8, 8), :]
-
-        @pl.when(fold_w == lon)
-        def _():
-            corner[3] = pack[pl.ds(rows - 8, 8), :]
-
-    @pl.when(jnp.logical_not(top))
-    def _():
-        for c in north:
-            c.start()
-
-    @pl.when(jnp.logical_not(low))
-    def _():
-        for c in south:
-            c.start()
-
     nclass = table.shape[1]
 
     def slopes(idx):
@@ -386,6 +323,70 @@
     over_chunks(1, rows // 8, GROUP, each(own_slopes))
     over_chunks(1, rows // 8, GROUP, each(own_strips))
     over_chunks(1, rows // 8 - 1, GROUP, each(functools.partial(coefs, range(own))))
+    others = lambda x: jnp.where(x, 1, 0)
+    count = 2 + 3 * others(jnp.logical_not(low)) + others(top) * (
+        1 + others(fold_e != lon) + others(fold_w != lon)) + 3 * others(jnp.logical_not(top))
+    pl.semaphore_wait(barrier, count)
+
+    pack_top = pack.at[pl.ds(rows - 8, 8), :]
+    pack_low = pack.at[pl.ds(0, 8), :]
+    from_west = col_t.at[pl.ds(HALF, PACKED), :]
+    from_east = col_t.at[pl.ds(0, PACKED), :]
+
+    def rdma(src, dst, s, r, a, o):
+        return pltpu.make_async_remote_copy(
+            src_ref=src, dst_ref=dst, send_sem=send_sem.at[s], recv_sem=recv_sem.at[r],
+            device_id=(o, a), device_id_type=MESH)
+
+    to_east = rdma(pack_t.at[pl.ds(HALF, PACKED), :], from_west, 0, 0, lat, east)
+    to_west = rdma(pack_t.at[pl.ds(0, PACKED), :], from_east, 1, 1, lat, west)
+    north = [
+        rdma(tops, sbuf, 2, 3, lat + 1, lon),
+        rdma(pack_top, corner.at[1], 3, 5, lat + 1, east),
+        rdma(pack_top, corner.at[0], 4, 4, lat + 1, west),
+    ]
+    mirror = rdma(tops, nbuf, 2, 2, lat, fold)
+    mirror_e = rdma(pack_top, corner.at[2], 3, 6, lat, fold_e)
+    mirror_w = rdma(pack_top, corner.at[3], 4, 7, lat, fold_w)
+    south = [
+        rdma(bots, nbuf, 5, 2, lat - 1, lon),
+        rdma(pack_low, corner.at[3], 6, 7, lat - 1, east),
+        rdma(pack_low, corner.at[2], 7, 6, lat - 1, west),
+    ]
+
+    to_east.start()
+    to_west.start()
+
+    @pl.when(top)
+    def _():
+        mirror.start()
+
+        @pl.when(fold_e != lon)
+        def _():
+            mirror_e.start()
+
+        @pl.when(fold_w != lon)
+        def _():
+            mirror_w.start()
+
+        @pl.when(fold_e == lon)
+        def _():
+            corner[2] = pack[pl.ds(rows - 8, 8), :]
+
+        @pl.when(fold_w == lon)
+        def _():
+            corner[3] = pack[pl.ds(rows - 8, 8), :]
+
+    @pl.when(jnp.logical_not(top))
+    def _():
+        for c in north:
+            c.start()
+
+    @pl.when(jnp.logical_not(low))
+    def _():
+        for c in south:
+            c.start()
+
     for step in range(STEPS):
         first = step + 2
         lat_only(step, first - 1)
@@ -474,7 +475,8 @@
         if last:
             lat_only(step, 0)
         ends = list(range(last, step + 2)) + list(range(chunks - step - 2, chunks - last))
-        advance(step, (0, 1), ends)
+        for j in range(0, len(ends), GROUP):
+            advance(step, (0, 1), ends[j:j + GROUP])
         over_chunks(0, chunks, STRIP_GROUP, functools.partial(advance, step, (2,)))
 
     def merge(e):
@@ -526,7 +528,7 @@
     vmem = pl.BlockSpec(memory_space=pltpu.VMEM)
     return pl.pallas_call(
         functools.partial(kernel, nlat, nlon),
-        out_shape=(jax.ShapeDtypeStruct((rows, cols), f32),) * 2,
+        out_shape=(pltpu.VMEM((rows, cols), f32),) * 2,
         in_specs=[any_, any_, any_, any_, pl.BlockSpec(memory_space=pltpu.SMEM), any_, any_],
         out_specs=(vmem, vmem),
         scratch_shapes=[
@@ -550,7 +552,7 @@
             pltpu.SemaphoreType.DMA((8,)),
         ],
         compiler_params=pltpu.CompilerParams(
-            collective_id=0, has_side_effects=True, vmem_limit_bytes=64 * 1024 * 1024 - 65536),
+            collective_id=0, has_side_effects=True, vmem_limit_bytes=VMEM_BYTES - 2 * rows * cols * 4 - 65536),
         name="tracer_steps",
     )(*args[:4], args[4].T, *args[5:])
 

time: 26.9 us -> 23.3 us (0.87)
  Pallas kernels: 23.7 us -> 21.1 us
  local copies, waits for them, and re-layouts: 2.42 us -> 1.41 us
    pallas_call x1, Pallas kernels: 23.7 us -> 21.1 us  [local(): pl.pallas_call(functools.partial(kernel, nlat, nlon), out_shape=(pltpu.VM...]
    unnamed x4 -> x2, local copies, waits for them, and re-layouts: 2.42 us -> 1.41 us
where the time goes in v5:
time: 23.3 us; the launch traced here: 23.2 us
  Pallas kernels  21.1 us (91%)
  local copies, waits for them, and re-layouts  1.41 us (6%)
  between operations  0.64 us (3%)
    pallas_call x1, Pallas kernels, local(): pl.pallas_call(functools.partial(kernel, nlat, nlon), out_shape=(pltpu.VM...  21.1 us
    unnamed x2, local copies, waits for them, and re-layouts  1.41 us

profile of v5, /device:TPU:1, one launch (start us, length us, event | category | flops | bytes accessed | tf_op | source)
XLA Modules:
  0.0 23.2 jit_solution(15032005557126234173)
XLA Ops:
  0.6 21.1 %tracer_steps.1 = (f32[256,256]{1,0:T(8,128)S(1)}, f32[256,256]{1,0:T(8,128)S(1)}) custom-call(f32[256,256]{1,0:T(8,128)} %t_in.1, f32[256,256]{1,0:T(8,128)} %s_in.1, s32[256,256]{1,0:T(8,128)} %m_in.1, s32[256,256]{1,0:T(8,128)} %k_in.1, f32[2,16]{1,0:T(2,128)} %bitcast.1, f32[256,256]{1,0:T(8,128)} %u_in.1, f32[256,256]{1,0:T(8,128)} %v_in.1), custom_call_target="tpu_custom_call" | custom-call | tf_op jit(solution)/shard_map/tracer_steps/pallas_call | solution.py:529
  21.8 0.7 %copy.11 = f32[256,256]{1,0:T(8,128)} copy(f32[256,256]{1,0:T(8,128)S(1)} %get-tuple-element.2) | data formatting | bytes 524288
  22.5 0.7 %copy.12 = f32[256,256]{1,0:T(8,128)} copy(f32[256,256]{1,0:T(8,128)S(1)} %get-tuple-element.3) | data formatting | bytes 524288

commit v6 on v5

--- a/solution.py
+++ b/solution.py
@@ -224,11 +224,9 @@
     def shifted(x, by):
         r = [pltpu.roll(a, (-by) % LANES, 1) for a in x]
         n = len(x)
-        if n == 1:
-            return r
         if by > 0:
-            return [jnp.where(lane >= LANES - by, r[(t + 1) % n], r[t]) for t in range(n)]
-        return [jnp.where(lane < -by, r[t - 1], r[t]) for t in range(n)]
+            return [jnp.where(lane >= LANES - by, r[t + 1], r[t]) for t in range(n - 1)] + r[-1:]
+        return r[:1] + [jnp.where(lane < -by, r[t - 1], r[t]) for t in range(1, n)]
 
     def coefs(tiles, e):
         r = row_of(PAD + e * 8)
@@ -269,14 +267,11 @@
         qm, q0, q1, q2 = around
         pair = [a + b for a, b in zip(q0, q1)]
         pe, pw = shifted(pair, 1), shifted(pair, -1)
-        res = []
         for t in range(len(q0)):
             dn = q1[t] - q0[t]
             lim = limited(dn, jnp.where(k[2][t] > 0, q0[t] - qm[t], q2[t] - q1[t]))
-            g = k[0][t] * dn + k[1][t] * (pe[t] - pw[t]) - (k[2][t] * q0[t] + k[3][t] * lim)
-            gy[step, f, t, pl.ds(r, 8), :] = g
-            res.append(g)
-        return res
+            gy[step, f, t, pl.ds(r, 8), :] = (
+                k[0][t] * dn + k[1][t] * (pe[t] - pw[t]) - (k[2][t] * q0[t] + k[3][t] * lim))
 
     def lat_only(step, e):
         r = row_of(PAD + e * 8)
@@ -284,45 +279,50 @@
         for f in range(2):
             lat_flux(step, f, r, k, q_rows(step, f, r))
 
-    def stepped(step, f, r, k, masked):
-        around = q_rows(step, f, r)
-        qm, q0, q1, q2 = around
+    def lon_and_sum(step, f, r, k, masked):
+        tiles = range(own if f < 2 else 1)
+        qm, q0, q1 = [[q[step, f, t, pl.ds(r + j, 8), :] for t in tiles] for j in (-1, 0, 1)]
         qe, qw, qf = shifted(q0, 1), shifted(q0, -1), shifted(q0, 2)
         vert = [a - b for a, b in zip(q1, qm)]
         ve = shifted(vert, 1)
         gx = []
-        for t in range(len(q0)):
+        for t in tiles:
             dn = qe[t] - q0[t]
             lim = limited(dn, jnp.where(k[2][t] > 0, q0[t] - qw[t], qf[t] - qe[t]))
             gx.append(k[0][t] * dn + k[1][t] * (vert[t] + ve[t]) - (k[2][t] * q0[t] + k[3][t] * lim))
         gw = shifted(gx, -1)
-        g = lat_flux(step, f, r, k[4:], around)
-        new = []
-        for t in range(len(q0)):
+        for t in tiles:
             centre = q0[t] * masked[t] if masked is not None else q0[t]
-            new.append(centre + (gx[t] - gw[t]) + g[t])
-        return new
+            value = (centre + (gx[t] - gw[t])) + (
+                gy[step, f, t, pl.ds(r, 8), :] - gy[step, f, t, pl.ds(r - 1, 8), :])
+            if step == STEPS - 1 and f < 2:
+                (t_out, s_out)[f][pl.ds(row_of(r - BASE), 8), pl.ds(LANES * t, LANES)] = value
+            else:
+                q[step + 1, f, t, pl.ds(r, 8), :] = value
 
     def advance(step, fields, group):
-        found = []
-        for e in group:
-            r = row_of(PAD + e * 8)
-            tiles = coef_tiles(fields[0])
-            k = [[coef[j, t, pl.ds(r, 8), :] for t in tiles] for j in range(8)]
+        tiles = coef_tiles(fields[0])
+        at = [row_of(PAD + e * 8) for e in group]
+        for r in at:
+            k = [[coef[j, t, pl.ds(r, 8), :] for t in tiles] for j in range(4, 8)]
+            for f in fields:
+                lat_flux(step, f, r, k, q_rows(step, f, r))
+        for r in at:
+            k = [[coef[j, t, pl.ds(r, 8), :] for t in tiles] for j in range(4)]
             masked = [stat[2, t, pl.ds(r, 8), :] for t in tiles] if step == 0 else None
             for f in fields:
-                found.append((f, r, stepped(step, f, r, k, masked)))
-        for f, r, new in found:
-            for t in range(len(new)):
-                value = new[t] - gy[step, f, t, pl.ds(r - 1, 8), :]
-                if step == STEPS - 1 and f < 2:
-                    (t_out, s_out)[f][pl.ds(row_of(r - BASE), 8), pl.ds(LANES * t, LANES)] = value
-                else:
-                    q[step + 1, f, t, pl.ds(r, 8), :] = value
+                lon_and_sum(step, f, r, k, masked)
 
     over_chunks(1, rows // 8, GROUP, each(own_slopes))
     over_chunks(1, rows // 8, GROUP, each(own_strips))
     over_chunks(1, rows // 8 - 1, GROUP, each(functools.partial(coefs, range(own))))
+    def interior(step):
+        first = step + 2
+        lat_only(step, first - 1)
+        over_chunks(first, chunks - 2 * first, GROUP, functools.partial(advance, step, (0, 1)))
+
+    interior(0)
+
     others = lambda x: jnp.where(x, 1, 0)
     count = 2 + 3 * others(jnp.logical_not(low)) + others(top) * (
         1 + others(fold_e != lon) + others(fold_w != lon)) + 3 * others(jnp.logical_not(top))
@@ -387,10 +387,8 @@
         for c in south:
             c.start()
 
-    for step in range(STEPS):
-        first = step + 2
-        lat_only(step, first - 1)
-        over_chunks(first, chunks - 2 * first, GROUP, functools.partial(advance, step, (0, 1)))
+    for step in range(1, STEPS):
+        interior(step)
 
     to_east.wait_recv()
     to_west.wait_recv()

time: 23.3 us -> 25.5 us (1.094)
  Pallas kernels: 21.1 us -> 23.3 us
    pallas_call x1, Pallas kernels: 21.1 us -> 23.3 us  [local(): pl.pallas_call(functools.partial(kernel, nlat, nlon), out_shape=(pltpu.VM...]
where the time goes in v6:
time: 25.5 us; the launch traced here: 25.3 us
  Pallas kernels  23.3 us (91%)
  local copies, waits for them, and re-layouts  1.41 us (6%)
  between operations  0.64 us (3%)
    pallas_call x1, Pallas kernels, local(): pl.pallas_call(functools.partial(kernel, nlat, nlon), out_shape=(pltpu.VM...  23.3 us
    unnamed x2, local copies, waits for them, and re-layouts  1.41 us

profile of v6, /device:TPU:1, one launch (start us, length us, event | category | flops | bytes accessed | tf_op | source)
XLA Modules:
  0.0 25.3 jit_solution(18279399443702321986)
XLA Ops:
  0.6 23.3 %tracer_steps.1 = (f32[256,256]{1,0:T(8,128)S(1)}, f32[256,256]{1,0:T(8,128)S(1)}) custom-call(f32[256,256]{1,0:T(8,128)} %t_in.1, f32[256,256]{1,0:T(8,128)} %s_in.1, s32[256,256]{1,0:T(8,128)} %m_in.1, s32[256,256]{1,0:T(8,128)} %k_in.1, f32[2,16]{1,0:T(2,128)} %bitcast.1, f32[256,256]{1,0:T(8,128)} %u_in.1, f32[256,256]{1,0:T(8,128)} %v_in.1), custom_call_target="tpu_custom_call" | custom-call | tf_op jit(solution)/shard_map/tracer_steps/pallas_call | solution.py:527
  23.9 0.7 %copy.11 = f32[256,256]{1,0:T(8,128)} copy(f32[256,256]{1,0:T(8,128)S(1)} %get-tuple-element.2) | data formatting | bytes 524288
  24.6 0.7 %copy.12 = f32[256,256]{1,0:T(8,128)} copy(f32[256,256]{1,0:T(8,128)S(1)} %get-tuple-element.3) | data formatting | bytes 524288

commit v7 on v5

--- a/solution.py
+++ b/solution.py
@@ -224,11 +224,9 @@
     def shifted(x, by):
         r = [pltpu.roll(a, (-by) % LANES, 1) for a in x]
         n = len(x)
-        if n == 1:
-            return r
         if by > 0:
-            return [jnp.where(lane >= LANES - by, r[(t + 1) % n], r[t]) for t in range(n)]
-        return [jnp.where(lane < -by, r[t - 1], r[t]) for t in range(n)]
+            return [jnp.where(lane >= LANES - by, r[t + 1], r[t]) for t in range(n - 1)] + r[-1:]
+        return r[:1] + [jnp.where(lane < -by, r[t - 1], r[t]) for t in range(1, n)]
 
     def coefs(tiles, e):
         r = row_of(PAD + e * 8)
@@ -322,7 +320,6 @@
 
     over_chunks(1, rows // 8, GROUP, each(own_slopes))
     over_chunks(1, rows // 8, GROUP, each(own_strips))
-    over_chunks(1, rows // 8 - 1, GROUP, each(functools.partial(coefs, range(own))))
     others = lambda x: jnp.where(x, 1, 0)
     count = 2 + 3 * others(jnp.logical_not(low)) + others(top) * (
         1 + others(fold_e != lon) + others(fold_w != lon)) + 3 * others(jnp.logical_not(top))
@@ -387,6 +384,7 @@
         for c in south:
             c.start()
 
+    over_chunks(1, rows // 8 - 1, GROUP, each(functools.partial(coefs, range(own))))
     for step in range(STEPS):
         first = step + 2
         lat_only(step, first - 1)

time: 23.3 us -> 23.3 us (level)
  no operation moved by 1% of the time
where the time goes in v7:
time: 23.3 us; the launch traced here: 23.1 us
  Pallas kernels  21.1 us (91%)
  local copies, waits for them, and re-layouts  1.41 us (6%)
  between operations  0.64 us (3%)
    pallas_call x1, Pallas kernels, local(): pl.pallas_call(functools.partial(kernel, nlat, nlon), out_shape=(pltpu.VM...  21.1 us
    unnamed x2, local copies, waits for them, and re-layouts  1.41 us

profile of v7, /device:TPU:1, one launch (start us, length us, event | category | flops | bytes accessed | tf_op | source)
XLA Modules:
  0.0 23.1 jit_solution(10784410553471164149)
XLA Ops:
  0.6 21.1 %tracer_steps.1 = (f32[256,256]{1,0:T(8,128)S(1)}, f32[256,256]{1,0:T(8,128)S(1)}) custom-call(f32[256,256]{1,0:T(8,128)} %t_in.1, f32[256,256]{1,0:T(8,128)} %s_in.1, s32[256,256]{1,0:T(8,128)} %m_in.1, s32[256,256]{1,0:T(8,128)} %k_in.1, f32[2,16]{1,0:T(2,128)} %bitcast.1, f32[256,256]{1,0:T(8,128)} %u_in.1, f32[256,256]{1,0:T(8,128)} %v_in.1), custom_call_target="tpu_custom_call" | custom-call | tf_op jit(solution)/shard_map/tracer_steps/pallas_call | solution.py:527
  21.7 0.7 %copy.11 = f32[256,256]{1,0:T(8,128)} copy(f32[256,256]{1,0:T(8,128)S(1)} %get-tuple-element.2) | data formatting | bytes 524288
  22.4 0.7 %copy.12 = f32[256,256]{1,0:T(8,128)} copy(f32[256,256]{1,0:T(8,128)S(1)} %get-tuple-element.3) | data formatting | bytes 524288

commit v8 on v7

--- a/solution.py
+++ b/solution.py
@@ -20,6 +20,7 @@
 
 
 GROUP = 4
+STEP_GROUP = 6
 STRIP_GROUP = 17
 
 
@@ -388,7 +389,7 @@
     for step in range(STEPS):
         first = step + 2
         lat_only(step, first - 1)
-        over_chunks(first, chunks - 2 * first, GROUP, functools.partial(advance, step, (0, 1)))
+        over_chunks(first, chunks - 2 * first, STEP_GROUP, functools.partial(advance, step, (0, 1)))
 
     to_east.wait_recv()
     to_west.wait_recv()

time: 23.3 us -> 24.6 us (1.056)
  Pallas kernels: 21.1 us -> 22.4 us
    pallas_call x1, Pallas kernels: 21.1 us -> 22.4 us  [local(): pl.pallas_call(functools.partial(kernel, nlat, nlon), out_shape=(pltpu.VM...]
where the time goes in v8:
time: 24.6 us; the launch traced here: 24.5 us
  Pallas kernels  22.4 us (91%)
  local copies, waits for them, and re-layouts  1.41 us (6%)
  between operations  0.64 us (3%)
    pallas_call x1, Pallas kernels, local(): pl.pallas_call(functools.partial(kernel, nlat, nlon), out_shape=(pltpu.VM...  22.4 us
    unnamed x2, local copies, waits for them, and re-layouts  1.41 us

profile of v8, /device:TPU:1, one launch (start us, length us, event | category | flops | bytes accessed | tf_op | source)
XLA Modules:
  0.0 24.5 jit_solution(11617990334030962673)
XLA Ops:
  0.6 22.4 %tracer_steps.1 = (f32[256,256]{1,0:T(8,128)S(1)}, f32[256,256]{1,0:T(8,128)S(1)}) custom-call(f32[256,256]{1,0:T(8,128)} %t_in.1, f32[256,256]{1,0:T(8,128)} %s_in.1, s32[256,256]{1,0:T(8,128)} %m_in.1, s32[256,256]{1,0:T(8,128)} %k_in.1, f32[2,16]{1,0:T(2,128)} %bitcast.1, f32[256,256]{1,0:T(8,128)} %u_in.1, f32[256,256]{1,0:T(8,128)} %v_in.1), custom_call_target="tpu_custom_call" | custom-call | tf_op jit(solution)/shard_map/tracer_steps/pallas_call | solution.py:528
  23.0 0.7 %copy.11 = f32[256,256]{1,0:T(8,128)} copy(f32[256,256]{1,0:T(8,128)S(1)} %get-tuple-element.2) | data formatting | bytes 524288
  23.7 0.7 %copy.12 = f32[256,256]{1,0:T(8,128)} copy(f32[256,256]{1,0:T(8,128)S(1)} %get-tuple-element.3) | data formatting | bytes 524288
